TPU v7x, 128 devices: a whole 4x4x4 slice. The times are simulated.
128 devices in a mesh: row: 16 (over z_lo, y, core), col: 8 (over z_hi, x).
Axes of the slice: x: 4, y: 4, z: 4 (z_hi: 2, z_lo: 2; z = z_hi * 2 + z_lo), core: 2. Of those that a mesh axis runs over, the one named last changes fastest.
Arguments:
- pair_act: bfloat16 [576, 576, 128], P('row', 'col'), may hold values from -6 to 6
- cotangent: bfloat16 [576, 576, 128], P('row', 'col'), may hold values from -6 to 6
- residue_mask: int32 [576], replicated, may hold values 0 or 1
- pair_mask: int32 [576, 576], P('row', 'col'), may hold values 0 or 1
- proj_weight: bfloat16 [128, 512], replicated, may hold values from -0.5 to 0.5
- gate_weight: bfloat16 [128, 128], replicated, may hold values from -0.5 to 0.5
- out_weight: bfloat16 [128, 128], replicated, may hold values from -0.5 to 0.5
- trans_in: bfloat16 [128, 1024], replicated, may hold values from -0.5 to 0.5
- trans_out: bfloat16 [512, 128], replicated, may hold values from -0.25 to 0.25
- norm_gains: float32 [3, 128], replicated, may hold values from 0.1 to 1.9
Outputs:
- grad_pair: bfloat16 [576, 576, 128], P('row', 'col')
- grad_proj: float32 [128, 512], replicated
- grad_gate: float32 [128, 128], replicated
- grad_out: float32 [128, 128], replicated
- grad_trans_in: float32 [128, 1024], replicated
- grad_trans_out: float32 [512, 128], replicated
- grad_gains: float32 [3, 128], replicated
All inputs are finite; a program needn't handle non-finite values. No bound on the sum of `pair_mask` on one device may be relied on, other than what follows from the above.
Results may differ from a plain program's by a relative error of at most 0.03.
Values may be sent and summed in bfloat16 or wider, within the bound.
A program may use at most 256 MiB of HBM per device.

v0:
```python
import jax
import jax.numpy as jnp
from jax import lax
from jax.sharding import PartitionSpec as P

EPSILON = 1e-05


def normalize(values):
    center = values - jnp.mean(values, axis=-1, keepdims=True)
    inverse = lax.rsqrt(jnp.mean(center * center, axis=-1, keepdims=True) + EPSILON)
    return (center * inverse, inverse)


def normalize_back(grad_hat, normed, inverse):
    mean_grad = jnp.mean(grad_hat, axis=-1, keepdims=True)
    second = jnp.mean(grad_hat * normed, axis=-1, keepdims=True)
    return inverse * (grad_hat - mean_grad - normed * second)


def over_rows(left_mat, right_mat):
    return lax.dot_general(
        left_mat, right_mat, (((0,), (0,)), ((), ())), preferred_element_type=jnp.float32
    )


def over_cols(left_mat, right_mat):
    return lax.dot_general(
        left_mat, right_mat, (((1,), (1,)), ((), ())), preferred_element_type=jnp.float32
    )


def project_in(pair_rows, mask_rows, proj_weight, gate_weight, gain_row):
    normed, inverse = normalize(pair_rows.astype(jnp.float32))
    scaled = (normed * gain_row).astype(jnp.bfloat16)
    projected = jnp.dot(scaled, proj_weight, preferred_element_type=jnp.float32)
    channels = gain_row.shape[0]
    left_sig = jax.nn.sigmoid(projected[:, :channels])
    right_sig = jax.nn.sigmoid(projected[:, 2 * channels : 3 * channels])
    left_val = (left_sig * projected[:, channels : 2 * channels] * mask_rows).astype(jnp.bfloat16)
    right_val = (right_sig * projected[:, 3 * channels :] * mask_rows).astype(jnp.bfloat16)
    gate_val = jax.nn.sigmoid(jnp.dot(scaled, gate_weight, preferred_element_type=jnp.float32))
    return (left_val, right_val, gate_val, projected, scaled, normed, inverse)


def project_out(mixed_rows, gate_val, pair_rows, out_weight, gain_row):
    normed, inverse = normalize(mixed_rows)
    scaled = (normed * gain_row).astype(jnp.bfloat16)
    output = jnp.dot(scaled, out_weight, preferred_element_type=jnp.float32)
    after_mix = (pair_rows.astype(jnp.float32) + gate_val * output).astype(jnp.bfloat16)
    return (after_mix, output, scaled, normed, inverse)


def transition_back(after_mix, cot_rows, trans_in, trans_out, gain_row):
    normed, inverse = normalize(after_mix.astype(jnp.float32))
    scaled = (normed * gain_row).astype(jnp.bfloat16)
    hidden = jnp.dot(scaled, trans_in, preferred_element_type=jnp.float32)
    expand = trans_out.shape[0]
    gate_part = hidden[:, :expand]
    up_part = hidden[:, expand:]
    sigmoid_gate = jax.nn.sigmoid(gate_part)
    swish_gate = gate_part * sigmoid_gate
    inner_act = (swish_gate * up_part).astype(jnp.bfloat16)
    grad_tout = over_rows(inner_act, cot_rows)
    grad_inner = over_cols(cot_rows, trans_out)
    grad_gatepart = grad_inner * up_part * sigmoid_gate * (1.0 + gate_part * (1.0 - sigmoid_gate))
    grad_uppart = grad_inner * swish_gate
    grad_hidden = jnp.concatenate([grad_gatepart, grad_uppart], axis=1).astype(jnp.bfloat16)
    grad_tin = over_rows(scaled, grad_hidden)
    grad_scaled = over_cols(grad_hidden, trans_in)
    grad_gain = jnp.sum(grad_scaled * normed, axis=0)
    grad_after = cot_rows.astype(jnp.float32) + normalize_back(
        grad_scaled * gain_row, normed, inverse
    )
    return (grad_after, grad_tin, grad_tout, grad_gain)


def output_back(grad_after, gate_val, output, scaled, normed, inverse, out_weight, gain_row):
    grad_output = (grad_after * gate_val).astype(jnp.bfloat16)
    grad_logit = (grad_after * output * gate_val * (1.0 - gate_val)).astype(jnp.bfloat16)
    grad_outw = over_rows(scaled, grad_output)
    grad_scaled = over_cols(grad_output, out_weight)
    grad_gain = jnp.sum(grad_scaled * normed, axis=0)
    grad_mixed = normalize_back(grad_scaled * gain_row, normed, inverse).astype(jnp.bfloat16)
    return (grad_mixed, grad_logit, grad_outw, grad_gain)


def input_back(
    grad_left,
    grad_right,
    grad_logit,
    grad_after,
    projected,
    mask_rows,
    scaled,
    normed,
    inverse,
    proj_weight,
    gate_weight,
    gain_row,
):
    channels = gain_row.shape[0]
    left_sig = jax.nn.sigmoid(projected[:, :channels])
    left_lin = projected[:, channels : 2 * channels]
    right_sig = jax.nn.sigmoid(projected[:, 2 * channels : 3 * channels])
    right_lin = projected[:, 3 * channels :]
    masked_left = grad_left * mask_rows
    masked_right = grad_right * mask_rows
    grad_proj = jnp.concatenate(
        [
            masked_left * left_lin * left_sig * (1.0 - left_sig),
            masked_left * left_sig,
            masked_right * right_lin * right_sig * (1.0 - right_sig),
            masked_right * right_sig,
        ],
        axis=1,
    ).astype(jnp.bfloat16)
    grad_projw = over_rows(scaled, grad_proj)
    grad_gatew = over_rows(scaled, grad_logit)
    grad_scaled = over_cols(grad_proj, proj_weight) + over_cols(grad_logit, gate_weight)
    grad_gain = jnp.sum(grad_scaled * normed, axis=0)
    grad_pair = (grad_after + normalize_back(grad_scaled * gain_row, normed, inverse)).astype(
        jnp.bfloat16
    )
    return (grad_pair, grad_projw, grad_gatew, grad_gain)


def on_device(
    pair_act,
    cotangent,
    residue_mask,
    pair_mask,
    proj_weight,
    gate_weight,
    out_weight,
    trans_in,
    trans_out,
    norm_gains,
):
    tile_rows, tile_cols, channels = pair_act.shape
    entries = tile_rows * tile_cols
    live_res = residue_mask.astype(jnp.float32)
    row_live = lax.dynamic_slice_in_dim(live_res, lax.axis_index("row") * tile_rows, tile_rows)
    col_live = lax.dynamic_slice_in_dim(live_res, lax.axis_index("col") * tile_cols, tile_cols)
    mask_rows = (pair_mask.astype(jnp.float32) * row_live[:, None] * col_live[None, :]).reshape(
        entries, 1
    )
    pair_rows = pair_act.reshape(entries, channels)
    cot_rows = cotangent.reshape(entries, channels)
    left_val, right_val, gate_val, projected, scaled_in, normed_in, inverse_in = project_in(
        pair_rows, mask_rows, proj_weight, gate_weight, norm_gains[0]
    )
    left_tile = left_val.reshape(tile_rows, tile_cols, channels)
    right_tile = right_val.reshape(tile_rows, tile_cols, channels)
    right_slab = lax.all_gather(right_tile, "row", axis=0, tiled=True)
    partial_value = jnp.einsum(
        "ikc,jkc->ijc", left_tile, right_slab, preferred_element_type=jnp.float32
    )
    mixed_tile = lax.psum_scatter(
        partial_value.astype(jnp.bfloat16), "col", scatter_dimension=1, tiled=True
    ).astype(jnp.float32)
    after_mix, output, scaled_out, normed_out, inverse_out = project_out(
        mixed_tile.reshape(entries, channels), gate_val, pair_rows, out_weight, norm_gains[1]
    )
    grad_after, grad_tin, grad_tout, gain_three = transition_back(
        after_mix, cot_rows, trans_in, trans_out, norm_gains[2]
    )
    grad_mixed, grad_logit, grad_outw, gain_two = output_back(
        grad_after, gate_val, output, scaled_out, normed_out, inverse_out, out_weight, norm_gains[1]
    )
    grad_tile = grad_mixed.reshape(tile_rows, tile_cols, channels)
    grad_row = lax.all_gather(grad_tile, "col", axis=1, tiled=True)
    grad_left = jnp.einsum("ijc,jkc->ikc", grad_row, right_slab, preferred_element_type=jnp.float32)
    grad_right = lax.psum_scatter(
        jnp.einsum("ijc,ikc->jkc", grad_row, left_tile, preferred_element_type=jnp.float32).astype(
            jnp.bfloat16
        ),
        "row",
        scatter_dimension=0,
        tiled=True,
    ).astype(jnp.float32)
    grad_pair, grad_projw, grad_gatew, gain_one = input_back(
        grad_left.reshape(entries, channels),
        grad_right.reshape(entries, channels),
        grad_logit,
        grad_after,
        projected,
        mask_rows,
        scaled_in,
        normed_in,
        inverse_in,
        proj_weight,
        gate_weight,
        norm_gains[0],
    )
    totals = lax.psum(
        (
            grad_projw,
            grad_gatew,
            grad_outw,
            grad_tin,
            grad_tout,
            jnp.stack([gain_one, gain_two, gain_three]),
        ),
        ("row", "col"),
    )
    residues = tile_rows * lax.axis_size("row")
    return (
        grad_pair.reshape(tile_rows, tile_cols, channels),
        totals[0] / residues,
        totals[1] / residues,
        totals[2] / residues,
        totals[3] / residues,
        totals[4] / residues,
        totals[5] / residues,
    )


def solution(mesh):
    in_specs = (
        P("row", "col", None),
        P("row", "col", None),
        P(),
        P("row", "col"),
        P(),
        P(),
        P(),
        P(),
        P(),
        P(),
    )
    out_specs = (P("row", "col", None), P(), P(), P(), P(), P(), P())
    return jax.shard_map(
        on_device, mesh=mesh, in_specs=in_specs, out_specs=out_specs, check_vma=False
    )
```

profile of v0, /device:TPU:1, one launch (start us, length us, event | category | flops | bytes accessed | tf_op | source)
XLA Modules:
  0.0 685.0 jit_solution(1463690261127174371)
XLA Ops:
  11.6 2.3 fusion.36
  15.6 2.6 multiply_convert_fusion.10
  19.7 64.9 %all-gather.3.cloned.1.call-done = bf16[576,72,128]{2,1,0:T(8,128)(2,1)} async-done(((bf16[36,72,128]{2,1,0:T(8,128)(2,1)}), bf16[576,72,128]{2,1,0:T(8,128)(2,1)}) %all-gather.3.cloned.1.call-update) | async-done | bytes 10616848 | tf_op jit(solution)/shard_map/all_gather | solution.py:155
  84.6 21.6 %copy.31 = bf16[576,72,128]{1,0,2:T(8,128)(2,1)} copy(bf16[576,72,128]{2,1,0:T(8,128)(2,1)} %all-gather.3.cloned.1.call-done) | data formatting | bytes 21233664 | tf_op jit(solution)/shard_map/all_gather | solution.py:155
  106.2 16.0 %fusion = bf16[36,576,128]{1,0,2:T(8,128)(2,1)} fusion(bf16[576,72,128]{1,0,2:T(8,128)(2,1)} %copy.31, bf16[36,72,128]{1,0,2:T(8,128)(2,1)S(1)} %copy.32), kind=kOutput, calls=%fused_computation.2 | convolution fusion | flops 384860160 | bytes 16588800 | tf_op jit(solution)/shard_map/ikc,jkc->ijc/dot_general | solution.py:156
  122.2 11.5 %copy.33 = bf16[36,576,128]{2,0,1:T(8,128)(2,1)} copy(bf16[36,576,128]{1,0,2:T(8,128)(2,1)} %fusion) | data formatting | bytes 10616832 | tf_op jit(solution)/shard_map/convert_element_type | solution.py:160
  133.9 96.0 %reduce-scatter.3.cloned.1.call-done = bf16[36,72,128]{2,0,1:T(8,128)(2,1)} async-done(((bf16[36,576,128]{2,0,1:T(8,128)(2,1)}), bf16[36,72,128]{2,0,1:T(8,128)(2,1)}) %reduce-scatter.3.cloned.1.call-update) | async-done | bytes 663568 | tf_op jit(solution)/shard_map/reduce_scatter | solution.py:159
  239.3 3.0 multiply_convert_fusion.2
  243.2 2.3 fusion.19
  245.5 3.0 multiply_convert_fusion.4
  250.6 2.9 multiply_convert_fusion.7
  253.5 79.5 %all-gather.5.cloned.1.call-done = bf16[36,576,128]{2,1,0:T(8,128)(2,1)} async-done(((bf16[36,72,128]{2,1,0:T(8,128)(2,1)}), bf16[36,576,128]{2,1,0:T(8,128)(2,1)}) %all-gather.5.cloned.1.call-update) | async-done | bytes 5308432 | tf_op jit(solution)/shard_map/all_gather | solution.py:172
  333.0 10.8 %copy.36 = bf16[36,576,128]{1,0,2:T(8,128)(2,1)} copy(bf16[36,576,128]{2,1,0:T(8,128)(2,1)} %all-gather.5.cloned.1.call-done) | data formatting | bytes 10616832 | tf_op jit(solution)/shard_map/all_gather | solution.py:172
  343.8 11.2 %convert_bitcast_fusion = bf16[576,72,128]{0,1,2:T(8,128)(2,1)} fusion(bf16[36,72,128]{1,0,2:T(8,128)(2,1)S(1)} %copy.32, bf16[36,576,128]{1,0,2:T(8,128)(2,1)} %copy.36), kind=kOutput, calls=%fused_computation | convolution fusion | flops 387514368 | bytes 16588800 | tf_op jit(solution)/shard_map/ijc,ikc->jkc/dot_general | solution.py:175
  355.1 17.2 %copy.40 = bf16[576,72,128]{2,1,0:T(8,128)(2,1)} copy(bf16[576,72,128]{0,1,2:T(8,128)(2,1)} %convert_bitcast_fusion) | data formatting | bytes 21233664 | tf_op jit(solution)/shard_map/convert_element_type | solution.py:175
  375.6 6.1 fusion.5
  381.8 6.5 fusion.7
  388.3 10.2 %convolution_bitcast_fusion = f32[36,72,128]{1,0,2:T(8,128)S(1)} fusion(bf16[576,72,128]{1,0,2:T(8,128)(2,1)} %copy.31, bf16[36,576,128]{1,0,2:T(8,128)(2,1)} %copy.36), kind=kOutput, calls=%fused_computation.18 | convolution fusion | flops 382205952 | bytes 17252352 | tf_op jit(solution)/shard_map/ijc,jkc->ikc/dot_general | solution.py:173
  400.5 45.7 %reduce-scatter.5.cloned.1.call-done = bf16[36,72,128]{2,1,0:T(8,128)(2,1)} async-done(((bf16[576,72,128]{2,1,0:T(8,128)(2,1)}), bf16[36,72,128]{2,1,0:T(8,128)(2,1)}) %reduce-scatter.5.cloned.1.call-update) | async-done | bytes 663568 | tf_op jit(solution)/shard_map/reduce_scatter | solution.py:174
  446.2 3.9 multiply_convert_fusion.6
  452.5 2.3 fusion.39
  456.7 68.0 %psum.47 = f32[3,128]{1,0:T(4,128)S(1)} all-reduce(f32[3,128]{1,0:T(4,128)S(1)} %pad_maximum_fusion.6), channel_id=1, replica_groups=mesh['row'=16,'col'=8] {'row','col'}, use_global_device_ids=true, to_apply=%region_22.0 | all-reduce | flops 384 | bytes 3072 | tf_op jit(solution)/shard_map/psum | solution.py:196
  525.3 4.4 add_convert_fusion
  529.7 141.6 %all-reduce.3.cloned.1.call-done = (f32[128,512]{1,0:T(8,128)}, f32[128,128]{1,0:T(8,128)}, f32[128,128]{1,0:T(8,128)}, f32[128,1024]{1,0:T(8,128)}, f32[512,128]{1,0:T(8,128)}) async-done(((f32[128,512]{1,0:T(8,128)}, f32[128,128]{1,0:T(8,128)}, f32[128,128]{1,0:T(8,128)}, f32[128,1024]{1,0:T(8,128)}, f32[512,128]{1,0:T(8,128)}), (f32[128,512]{1,0:T(8,128)}, f32[128,128]{1,0:T(8,128)}, ...) | async-done | bytes 1179664 | tf_op jit(solution)/shard_map/psum | solution.py:196
  (156 shorter events, 37.2 us)
Async XLA Ops:
  7.2 230.5 %copy-start = (bf16[128,1024]{1,0:T(8,128)(2,1)S(1)}, bf16[128,1024]{1,0:T(8,128)(2,1)}, u32[]{:S(2)}) copy-start(bf16[128,1024]{1,0:T(8,128)(2,1)} %param.17) | copy-start | bytes 786436
  7.2 4.4 copy-start.4
  7.2 3.9 copy-start.44
  7.2 3.9 copy-start.43
  7.2 4.1 copy-start.40
  7.2 77.4 %all-gather.3.cloned.1.call-start = ((), (), s32[]{:S(2)}) async-start(), calls=%async_computation.2 | async-start | bytes 11280384 | tf_op jit(solution)/shard_map/all_gather | solution.py:155
  8.9 5.0 copy-start.27
  11.1 234.4 %copy-start.41 = (f32[128]{0:T(128)}, f32[128]{0:T(128)S(1)}, u32[]{:S(2)}) copy-start(f32[128]{0:T(128)S(1)} %get-tuple-element.35) | copy-start | bytes 1540
  11.4 4.1 copy-start.36
  11.6 3.2 copy-start.33
  15.6 2.6 copy-start.2
  18.2 211.8 %reduce-scatter.3.cloned.1.call-start = ((), (), s32[]{:S(2)}) async-start(), calls=%async_computation.3 | async-start | bytes 6635520 | tf_op jit(solution)/shard_map/reduce_scatter | solution.py:159
  133.7 199.3 %all-gather.5.cloned.1.call-start = ((), (), s32[]{:S(2)}) async-start(), calls=%async_computation.4 | async-start | bytes 5971968 | tf_op jit(solution)/shard_map/all_gather | solution.py:172
  236.5 8.9 %copy-start.7 = (bf16[2592,128]{1,0:T(8,128)(2,1)}, bf16[2592,128]{1,0:T(8,128)(2,1)S(1)}, u32[]{:S(2)}) copy-start(bf16[2592,128]{1,0:T(8,128)(2,1)S(1)} %get-tuple-element.38) | copy-start | bytes 1990660
  236.8 8.6 %copy-start.25 = (f32[2592]{0:T(1024)}, f32[2592]{0:T(1024)S(1)}, u32[]{:S(2)}) copy-start(f32[2592]{0:T(1024)S(1)} %broadcast_multiply_fusion.13) | copy-start | bytes 31108
  237.7 7.8 %copy-start.31 = (f32[2592]{0:T(1024)}, f32[2592]{0:T(1024)S(1)}, u32[]{:S(2)}) copy-start(f32[2592]{0:T(1024)S(1)} %add_rsqrt_fusion.2) | copy-start | bytes 31108
  239.3 3.9 copy-start.3
  253.5 192.7 %reduce-scatter.5.cloned.1.call-start = ((), (), s32[]{:S(2)}) async-start(), calls=%async_computation.5 | async-start | bytes 11280384 | tf_op jit(solution)/shard_map/reduce_scatter | solution.py:174
  372.2 299.0 %all-reduce.3.cloned.1.call-start = ((), (), s32[]{:S(2)}) async-start(), calls=%async_computation.6 | async-start | bytes 2359296 | tf_op jit(solution)/shard_map/psum | solution.py:196
  375.6 6.1 copy-start.21
  398.5 47.7 %copy-start.37 = (f32[2592]{0:T(1024)S(1)}, f32[2592]{0:T(1024)}, u32[]{:S(2)}) copy-start(f32[2592]{0:T(1024)} %copy-done.36) | copy-start | bytes 31108
  454.9 70.4 %copy-start.10 = (f32[2592,128]{1,0:T(8,128)S(1)}, f32[2592,128]{1,0:T(8,128)}, u32[]{:S(2)}) copy-start(f32[2592,128]{1,0:T(8,128)} %copy-done.9) | copy-start | bytes 3981316
  525.3 153.2 %copy-start.1 = (bf16[128,1024]{1,0:T(8,128)(2,1)S(1)}, bf16[128,1024]{1,0:T(8,128)(2,1)}, u32[]{:S(2)}) copy-start(bf16[128,1024]{1,0:T(8,128)(2,1)} %param.17) | copy-start | bytes 786436
  671.3 6.4 copy-start.24
  (30 other events, 48.1 us)
Sparse Core Ops, SparseCore 0:
  18.3 66.2 all-gather.2
  133.8 96.0 reduce-scatter.2
  253.6 79.3 all-gather.4
  372.4 73.7 reduce-scatter.4
  525.4 145.8 all-reduce.2
where the time goes:
time: 687 us; the launch traced here: 685 us
  waiting for transfers between devices  428 us (62%)
  local copies, waits for them, and re-layouts  70.8 us (10%)
  blocking collectives  68 us (10%)
  matrix products  67.1 us (10%)
  other arithmetic  36.3 us (5%)
  between operations  14.4 us (2%)
    psum x1, waiting for transfers between devices, on_device(): lax.psum((grad_projw, grad_gatew, grad_outw, grad_tin, grad_tout, jnp.sta...  142 us
    reduce_scatter x1, waiting for transfers between devices, on_device(): lax.psum_scatter(partial_value.astype(jnp.bfloat16), 'col', scatter_dimen...  96 us
    all_gather x1, waiting for transfers between devices, on_device(): grad_row = lax.all_gather(grad_tile, 'col', axis=1, tiled=True)  79.5 us
    psum x1, blocking collectives, on_device(): lax.psum((grad_projw, grad_gatew, grad_outw, grad_tin, grad_tout, jnp.sta...  68 us
    all_gather x1, waiting for transfers between devices, on_device(): right_slab = lax.all_gather(right_tile, 'row', axis=0, tiled=True)  64.9 us
    reduce_scatter x1, waiting for transfers between devices, on_device(): lax.psum_scatter(jnp.einsum('ijc,ikc->jkc', grad_row, left_tile, preferre...  45.7 us
    all_gather x1, local copies, waits for them, and re-layouts, on_device(): right_slab = lax.all_gather(right_tile, 'row', axis=0, tiled=True)  21.6 us
    convert_element_type x1, local copies, waits for them, and re-layouts, on_device(): jnp.einsum('ijc,ikc->jkc', grad_row, left_tile, preferred_element_type=jn...  17.2 us
  transfers between devices with their start and end apart: 5, of which 5 were waited for; matrix products, arithmetic and copies ran while one was open for 5% of the time, Pallas kernels for 0%

commit v1 on v0

v1 whole, which is shorter than its diff:
```python
import functools

import jax
import jax.numpy as jnp
from jax import lax
from jax.experimental import pallas as pl
from jax.experimental.pallas import tpu as pltpu
from jax.sharding import PartitionSpec as P

EPSILON = 1e-05
BF = jnp.bfloat16
F32 = jnp.float32
MESH = pl.DeviceIdType.MESH
C = 128
NR, NQ = 16, 8
ND = NR * NQ
TI, TK = 36, 72
E = TI * TK
NT = 21
EP = NT * 128
MROWS = TI * NR
KP = NQ * 128
CH = 384
STEPS = EP // CH
LR_T, MX_T = 48, 32
VMEM_LIMIT = 56 * 2**20


def vspec(n):
    return [pl.BlockSpec(memory_space=pltpu.VMEM)] * n


def sds(shape, dtype):
    return jax.ShapeDtypeStruct(shape, dtype)


def sigmoid(v):
    return 0.5 * jnp.tanh(0.5 * v) + 0.5


def norm(v):
    center = v - jnp.mean(v, axis=0, keepdims=True)
    inverse = lax.rsqrt(jnp.mean(center * center, axis=0, keepdims=True) + EPSILON)
    return center * inverse, inverse


def norm_back(h, n, inverse):
    first = jnp.mean(h, axis=0, keepdims=True)
    second = jnp.mean(h * n, axis=0, keepdims=True)
    return inverse * (h - first - n * second)


def mm(a, b):
    return jnp.dot(a, b, preferred_element_type=F32)


def mm_nt(a, b):
    return lax.dot_general(a, b, (((1,), (1,)), ((), ())), preferred_element_type=F32)


def eye():
    return (
        lax.broadcasted_iota(jnp.int32, (C, C), 0) == lax.broadcasted_iota(jnp.int32, (C, C), 1)
    ).astype(BF)


def load_t(ref, off, last):
    if last:
        rows = ref[(STEPS - 1) * CH : E, :]
        rows = jnp.concatenate([rows, jnp.zeros((EP - E, C), rows.dtype)], axis=0)
    else:
        rows = ref[pl.ds(off, CH), :]
    return mm_nt(eye(), rows)


def each_step(body):
    def loop(step, carry):
        body(step, pl.multiple_of(step * CH, CH), False)
        return carry

    lax.fori_loop(0, STEPS - 1, loop, 0)
    body(STEPS - 1, (STEPS - 1) * CH, True)


def gather_rows(ref, base, stride, count):
    return [ref[pl.ds(base + 8 * g * stride, 8, stride=stride), :] for g in range(count // 8)]


def project_kernel(x_ref, live_ref, w_ref, gain_ref, lr_ref, f_ref):
    f_ref[2 * NT * C :, :] = jnp.zeros(((LR_T - 2 * NT) * C, 128), F32)

    def body(step, off, last):
        normed, _ = norm(load_t(x_ref, off, last))
        scaled = (normed * gain_ref[:, 0:1]).astype(BF)
        proj = mm(w_ref[...], scaled)
        live = live_ref[0:1, pl.ds(off, CH)]
        left = sigmoid(proj[0:C]) * proj[C : 2 * C] * live
        right = sigmoid(proj[2 * C : 3 * C]) * proj[3 * C :] * live
        for tt in range(CH // 128):
            t = step * (CH // 128) + tt
            f_ref[pl.ds(t * C, C), :] = left[:, tt * 128 : (tt + 1) * 128]
            f_ref[pl.ds((NT + t) * C, C), :] = right[:, tt * 128 : (tt + 1) * 128]

    each_step(body)

    def out(c, carry):
        lr_ref[c] = jnp.concatenate(gather_rows(f_ref, c, C, LR_T), axis=0).astype(BF)
        return carry

    lax.fori_loop(0, C, out, 0)


def project(x, live, w, gains):
    return pl.pallas_call(
        project_kernel,
        out_shape=sds((C, LR_T, 128), BF),
        in_specs=vspec(4),
        out_specs=pl.BlockSpec(memory_space=pltpu.VMEM),
        scratch_shapes=[pltpu.VMEM((LR_T * C, 128), F32)],
        compiler_params=pltpu.CompilerParams(vmem_limit_bytes=VMEM_LIMIT),
        name="project",
    )(x, live, w, gains)


def middle_kernel(
    x_ref, cot_ref, mix_ref, wg_ref, wo_ref, wot_ref, ti_ref, tit_ref, to_ref, gain_ref,
    g_ref, after_ref, logit_ref, mid_ref,
    f_ref, fo_ref, tin_ref, tout_ref, ow_ref, gw_ref, gn_ref,
):
    H = to_ref.shape[0]

    def unpack(c, carry):
        f_ref[pl.ds(pl.multiple_of(c * MX_T, MX_T), MX_T), :] = mix_ref[c].astype(F32)
        return carry

    lax.fori_loop(0, C, unpack, 0)
    for ref in (tin_ref, tout_ref, ow_ref, gw_ref, gn_ref):
        ref[...] = jnp.zeros_like(ref)
    fo_ref[...] = jnp.zeros_like(fo_ref)

    def body(step, off, last):
        lanes = pl.ds(off, CH)
        x = load_t(x_ref, off, last)
        cot = load_t(cot_ref, off, last)
        cot_b = cot.astype(BF)
        normed_in, _ = norm(x)
        scaled_in = (normed_in * gain_ref[:, 0:1]).astype(BF)
        gate = sigmoid(mm(wg_ref[...], scaled_in))
        mixed = jnp.concatenate(
            [
                jnp.concatenate(gather_rows(f_ref, step * (CH // 128) + tt, MX_T, C), axis=0)
                for tt in range(CH // 128)
            ],
            axis=1,
        )
        normed_x, r_x = norm(mixed)
        scaled_out = (normed_x * gain_ref[:, 1:2]).astype(BF)
        output = mm(wot_ref[...], scaled_out)
        after = (x + gate * output).astype(BF).astype(F32)
        normed_t, r_t = norm(after)
        scaled_t = (normed_t * gain_ref[:, 2:3]).astype(BF)
        hidden = mm(tit_ref[...], scaled_t)
        gpart, upart = hidden[:H], hidden[H:]
        sg = sigmoid(gpart)
        swish = gpart * sg
        inner = (swish * upart).astype(BF)
        tout_ref[...] += mm_nt(inner, cot_b)
        grad_inner = mm(to_ref[...], cot_b)
        grad_hidden = jnp.concatenate(
            [
                (grad_inner * upart * sg * (1.0 + gpart * (1.0 - sg))).astype(BF),
                (grad_inner * swish).astype(BF),
            ],
            axis=0,
        )
        tin_ref[...] += mm_nt(scaled_t, grad_hidden)
        back_t = mm(ti_ref[...], grad_hidden)
        gn_ref[1] += back_t * normed_t
        grad_after = cot + norm_back(back_t * gain_ref[:, 2:3], normed_t, r_t)
        after_ref[:, lanes] = grad_after
        grad_output = (grad_after * gate).astype(BF)
        grad_logit = (grad_after * output * gate * (1.0 - gate)).astype(BF)
        logit_ref[:, lanes] = grad_logit
        gw_ref[...] += mm_nt(scaled_in, grad_logit)
        ow_ref[...] += mm_nt(scaled_out, grad_output)
        back_x = mm(wo_ref[...], grad_output)
        gn_ref[0] += back_x * normed_x
        grad_mixed = norm_back(back_x * gain_ref[:, 1:2], normed_x, r_x)
        for tt in range(CH // 128):
            t = step * (CH // 128) + tt
            for g in range(C // 8):
                fo_ref[pl.ds(t + 8 * g * MX_T, 8, stride=MX_T), :] = grad_mixed[
                    8 * g : 8 * g + 8, tt * 128 : (tt + 1) * 128
                ]

    each_step(body)

    def out(c, carry):
        g_ref[c] = fo_ref[pl.ds(pl.multiple_of(c * MX_T, MX_T), MX_T), :].astype(BF)
        return carry

    lax.fori_loop(0, C, out, 0)
    for b in range(2 * H // C):
        mid_ref[b * C : (b + 1) * C, :] = tin_ref[:, b * C : (b + 1) * C].astype(BF)
    base = 2 * H
    mid_ref[base : base + H, :] = tout_ref[...].astype(BF)
    base += H
    mid_ref[base : base + C, :] = ow_ref[...].astype(BF)
    mid_ref[base + C : base + 2 * C, :] = gw_ref[...].astype(BF)
    base += 2 * C
    mid_ref[base:, :] = jnp.zeros((mid_ref.shape[0] - base, 128), BF)
    rows = [jnp.sum(gn_ref[k].T, axis=0, keepdims=True) for k in range(2)]
    mid_ref[base : base + 16, :] = jnp.concatenate(rows + [jnp.zeros((14, 128), F32)], axis=0).astype(BF)


def middle(x, cot, mix, wg, wo, wot, ti, tit, to, gains):
    return pl.pallas_call(
        middle_kernel,
        out_shape=(sds((C, MX_T, 128), BF), sds((C, EP), F32), sds((C, EP), BF), sds((ND * 16, 128), BF)),
        in_specs=vspec(10),
        out_specs=tuple(vspec(4)),
        scratch_shapes=[
            pltpu.VMEM((MX_T * C, 128), F32),
            pltpu.VMEM((MX_T * C, 128), F32),
            pltpu.VMEM(ti.shape, F32),
            pltpu.VMEM(to.shape, F32),
            pltpu.VMEM((C, C), F32),
            pltpu.VMEM((C, C), F32),
            pltpu.VMEM((2, C, CH), F32),
        ],
        compiler_params=pltpu.CompilerParams(vmem_limit_bytes=VMEM_LIMIT),
        name="middle",
    )(x, cot, mix, wg, wo, wot, ti, tit, to, gains)


def last_kernel(
    x_ref, live_ref, back_ref, logit_ref, after_ref, wt_ref, w_ref, gain_ref,
    pair_ref, tail_ref,
    f_ref, pw_ref, gn_ref,
):
    def unpack(c, carry):
        f_ref[pl.ds(pl.multiple_of(c * LR_T, LR_T), LR_T), :] = back_ref[c].astype(F32)
        return carry

    lax.fori_loop(0, C, unpack, 0)
    pw_ref[...] = jnp.zeros_like(pw_ref)
    gn_ref[...] = jnp.zeros_like(gn_ref)

    def body(step, off, last):
        lanes = pl.ds(off, CH)
        normed, inverse = norm(load_t(x_ref, off, last))
        scaled = (normed * gain_ref[:, 0:1]).astype(BF)
        proj = mm(wt_ref[...], scaled)
        live = live_ref[0:1, lanes]

        def load(base):
            return live * jnp.concatenate(
                [
                    jnp.concatenate(gather_rows(f_ref, base + step * (CH // 128) + tt, LR_T, C), axis=0)
                    for tt in range(CH // 128)
                ],
                axis=1,
            )

        gl, gr = load(0), load(NT)
        s1, s3 = sigmoid(proj[0:C]), sigmoid(proj[2 * C : 3 * C])
        grad_proj = jnp.concatenate(
            [
                (gl * proj[C : 2 * C] * s1 * (1.0 - s1)).astype(BF),
                (gl * s1).astype(BF),
                (gr * proj[3 * C :] * s3 * (1.0 - s3)).astype(BF),
                (gr * s3).astype(BF),
            ],
            axis=0,
        )
        pw_ref[...] += mm_nt(scaled, grad_proj)
        back = mm(w_ref[...], jnp.concatenate([grad_proj, logit_ref[:, lanes]], axis=0))
        gn_ref[...] += back * normed
        grad = after_ref[:, lanes] + norm_back(back * gain_ref[:, 0:1], normed, inverse)
        rows = grad.T.astype(BF)
        if last:
            pair_ref[(STEPS - 1) * CH : E, :] = rows[: E - (STEPS - 1) * CH]
        else:
            pair_ref[pl.ds(off, CH), :] = rows

    each_step(body)
    for b in range(4):
        tail_ref[b * C : (b + 1) * C, :] = pw_ref[:, b * C : (b + 1) * C].astype(BF)
    tail_ref[4 * C :, :] = jnp.zeros((tail_ref.shape[0] - 4 * C, 128), BF)
    tail_ref[4 * C : 4 * C + 16, :] = jnp.concatenate(
        [jnp.sum(gn_ref[...].T, axis=0, keepdims=True), jnp.zeros((15, 128), F32)], axis=0
    ).astype(BF)


def last(x, live, back, logit, after, wt, w, gains):
    return pl.pallas_call(
        last_kernel,
        out_shape=(sds((E, C), BF), sds((ND * 16, 128), BF)),
        in_specs=vspec(8),
        out_specs=tuple(vspec(2)),
        scratch_shapes=[
            pltpu.VMEM((LR_T * C, 128), F32),
            pltpu.VMEM((C, 4 * C), F32),
            pltpu.VMEM((C, CH), F32),
        ],
        compiler_params=pltpu.CompilerParams(vmem_limit_bytes=VMEM_LIMIT),
        name="last",
    )(x, live, back, logit, after, wt, w, gains)


def each_peer(fn):
    r, q = lax.axis_index("row"), lax.axis_index("col")

    def one(pr, dq):
        fn(pr, lax.rem(q + dq, NQ))

    for dq in range(1, NQ):
        one(r, dq)

    def body(dr, carry):
        pr = lax.rem(r + dr, NR)
        for dq in range(NQ):
            one(pr, dq)
        return carry

    lax.fori_loop(1, NR, body, 0)


def entry_barrier():
    barrier = pltpu.get_barrier_semaphore()
    each_peer(
        lambda pr, pq: pl.semaphore_signal(barrier, inc=1, device_id=(pr, pq), device_id_type=MESH)
    )
    pl.semaphore_wait(barrier, ND - 1)


def exchange_start(src, dst, src_slot, dst_slot, sems):
    r, q = lax.axis_index("row"), lax.axis_index("col")
    mine = dst_slot(r, q)

    def send(pr, pq):
        pltpu.make_async_remote_copy(
            src_ref=src.at[src_slot(pr, pq)],
            dst_ref=dst.at[mine],
            send_sem=sems.at[0],
            recv_sem=sems.at[1],
            device_id=(pr, pq),
            device_id_type=MESH,
        ).start()

    each_peer(send)
    pltpu.make_async_copy(src.at[src_slot(r, q)], dst.at[mine], sems.at[2]).start()


def exchange_wait(src, dst, sems):
    part = pl.ds(0, ND - 1)
    pltpu.make_async_copy(src.at[part], dst.at[part], sems.at[1]).wait()
    pltpu.make_async_copy(src.at[0], dst.at[0], sems.at[2]).wait()


def exchange_wait_send(src, dst, sems):
    part = pl.ds(0, ND - 1)
    pltpu.make_async_copy(src.at[part], dst.at[part], sems.at[0]).wait()


def by_channel(r, q):
    return r * NQ + q


def by_entry(r, q):
    return q * NR + r


def widen(src, f_ref, rows):
    def body(s, carry):
        f_ref[pl.ds(pl.multiple_of(s * rows, rows), rows), :] = src[s].astype(F32)
        return carry

    lax.fori_loop(0, ND, body, 0)


def narrow(f_ref, dst, rows):
    def body(s, carry):
        dst[s] = f_ref[pl.ds(pl.multiple_of(s * rows, rows), rows), :].astype(BF)
        return carry

    lax.fori_loop(0, ND, body, 0)


def lane_iota():
    return lax.broadcasted_iota(jnp.int32, (8, 128), 1)


def roll(v, shift):
    shift %= 128
    return v if shift == 0 else pltpu.roll(v, shift, 1)


def split_rows(tiles):
    lane = lane_iota()
    for ii in range(TI):
        t, l = divmod(TK * ii, 128)
        v = tiles[t]
        if l + TK > 128:
            v = jnp.where(lane >= l, v, tiles[t + 1])
        yield ii, jnp.where(lane < TK, roll(v, -l), 0.0)


def join_rows(rows):
    lane = lane_iota()
    rolled = {}
    for t in range(NT):
        first = (128 * t) // TK
        final = min((128 * t + 127) // TK, TI - 1)
        value = jnp.zeros((8, 128), F32)
        for ii in range(final, first - 1, -1):
            start = TK * ii - 128 * t
            if ii not in rolled:
                rolled[ii] = roll(rows(ii), start)
            if ii == final and start + TK < 128:
                value = jnp.where(lane < start + TK, rolled[ii], value)
            elif ii == final:
                value = rolled[ii]
            else:
                value = jnp.where(lane < start + TK, rolled[ii], value)
        yield t, value


def triangle_kernel(lr_ref, mix_ref, l_ref, r_ref, in_ref, f_ref, rf_ref, c_ref, out_ref, sem_a, sem_b):
    entry_barrier()
    exchange_start(lr_ref, in_ref, by_channel, by_entry, sem_a)
    rf_ref[...] = jnp.zeros_like(rf_ref)
    exchange_wait(lr_ref, in_ref, sem_a)
    widen(in_ref, f_ref, LR_T)

    def per_col(q, carry):
        lanes = pl.ds(pl.multiple_of(q * 128, 128), 128)
        halves = []
        for h in range(2):
            base = (q * NR + 8 * h) * LR_T
            tiles = [f_ref[pl.ds(base + t, 8, stride=LR_T), :] for t in range(NT)]
            halves.append([v for _, v in split_rows(tiles)])
        for ii in range(TI):
            l_ref[ii * NR : (ii + 1) * NR, lanes] = jnp.concatenate(
                [halves[0][ii], halves[1][ii]], axis=0
            ).astype(BF)
        for h in range(2):
            base = (q * NR + h) * LR_T + NT
            tiles = [f_ref[pl.ds(base + t, 8, stride=2 * LR_T), :] for t in range(NT)]
            for jj, v in split_rows(tiles):
                rf_ref[pl.ds(h * TI + jj, 8, stride=128), :] = v
        r_ref[:, lanes] = rf_ref[...].astype(BF)
        return carry

    lax.fori_loop(0, NQ, per_col, 0)

    def product(b, carry):
        rows = pl.ds(pl.multiple_of(b * 128, 128), 128)
        c_ref[:, rows] = mm_nt(l_ref[...], r_ref[rows, :])
        return carry

    lax.fori_loop(0, NQ, product, 0)

    def pack(q, carry):
        lanes = pl.ds(pl.multiple_of(q * 128, 128), 128)
        for h in range(2):
            for t, v in join_rows(lambda ii: c_ref[ii * NR + 8 * h : ii * NR + 8 * h + 8, lanes]):
                f_ref[pl.ds((q * NR + 8 * h) * MX_T + t, 8, stride=MX_T), :] = v
        return carry

    lax.fori_loop(0, NQ, pack, 0)
    narrow(f_ref, out_ref, MX_T)
    exchange_start(out_ref, mix_ref, by_entry, by_channel, sem_b)
    exchange_wait_send(lr_ref, in_ref, sem_a)
    exchange_wait(out_ref, mix_ref, sem_b)
    exchange_wait_send(out_ref, mix_ref, sem_b)


def triangle(lr):
    return pl.pallas_call(
        triangle_kernel,
        out_shape=(sds((C, MX_T, 128), BF), sds((MROWS, KP), BF), sds((KP, KP), BF)),
        in_specs=vspec(1),
        out_specs=tuple(vspec(3)),
        scratch_shapes=[
            pltpu.VMEM((ND, LR_T, 128), BF),
            pltpu.VMEM((ND * LR_T, 128), F32),
            pltpu.VMEM((KP, 128), F32),
            pltpu.VMEM((MROWS, KP), F32),
            pltpu.VMEM((ND, MX_T, 128), BF),
            pltpu.SemaphoreType.DMA((3,)),
            pltpu.SemaphoreType.DMA((3,)),
        ],
        compiler_params=pltpu.CompilerParams(
            collective_id=1, has_side_effects=True, vmem_limit_bytes=VMEM_LIMIT
        ),
        name="triangle",
    )(lr)


def triangle_back_kernel(g_ref, l_ref, r_ref, back_ref, in_ref, f_ref, m_ref, c1_ref, c2_ref, out_ref, sem_a, sem_b):
    entry_barrier()
    exchange_start(g_ref, in_ref, by_channel, by_entry, sem_a)
    exchange_wait(g_ref, in_ref, sem_a)
    widen(in_ref, f_ref, MX_T)

    def per_col(q, carry):
        lanes = pl.ds(pl.multiple_of(q * 128, 128), 128)
        halves = []
        for h in range(2):
            base = (q * NR + 8 * h) * MX_T
            tiles = [f_ref[pl.ds(base + t, 8, stride=MX_T), :] for t in range(NT)]
            halves.append([v for _, v in split_rows(tiles)])
        for ii in range(TI):
            m_ref[ii * NR : (ii + 1) * NR, lanes] = jnp.concatenate(
                [halves[0][ii], halves[1][ii]], axis=0
            ).astype(BF)
        return carry

    lax.fori_loop(0, NQ, per_col, 0)

    def product(b, carry):
        lanes = pl.ds(pl.multiple_of(b * 128, 128), 128)
        c1_ref[:, lanes] = mm(m_ref[...], r_ref[:, lanes])
        c2_ref[pl.ds(pl.multiple_of(b * KP, KP), KP), :] = lax.dot_general(
            m_ref[...], l_ref[:, lanes], (((0,), (0,)), ((), ())), preferred_element_type=F32
        )
        return carry

    lax.fori_loop(0, NQ, product, 0)

    def pack(q, carry):
        lanes = pl.ds(pl.multiple_of(q * 128, 128), 128)
        for h in range(2):
            for t, v in join_rows(lambda ii: c1_ref[ii * NR + 8 * h : ii * NR + 8 * h + 8, lanes]):
                f_ref[pl.ds((q * NR + 8 * h) * LR_T + t, 8, stride=LR_T), :] = v
            for t, v in join_rows(lambda jj: c2_ref[pl.ds(q * KP + h * TI + jj, 8, stride=128), :]):
                f_ref[pl.ds((q * NR + h) * LR_T + NT + t, 8, stride=2 * LR_T), :] = v
        return carry

    lax.fori_loop(0, NQ, pack, 0)
    narrow(f_ref, out_ref, LR_T)
    exchange_start(out_ref, back_ref, by_entry, by_channel, sem_b)
    exchange_wait_send(g_ref, in_ref, sem_a)
    exchange_wait(out_ref, back_ref, sem_b)
    exchange_wait_send(out_ref, back_ref, sem_b)


def triangle_back(g, lmat, rmat):
    return pl.pallas_call(
        triangle_back_kernel,
        out_shape=sds((C, LR_T, 128), BF),
        in_specs=vspec(3),
        out_specs=pl.BlockSpec(memory_space=pltpu.VMEM),
        scratch_shapes=[
            pltpu.VMEM((ND, MX_T, 128), BF),
            pltpu.VMEM((ND * LR_T, 128), F32),
            pltpu.VMEM((MROWS, KP), BF),
            pltpu.VMEM((MROWS, KP), F32),
            pltpu.VMEM((NQ * KP, 128), F32),
            pltpu.VMEM((ND, LR_T, 128), BF),
            pltpu.SemaphoreType.DMA((3,)),
            pltpu.SemaphoreType.DMA((3,)),
        ],
        compiler_params=pltpu.CompilerParams(
            collective_id=2, has_side_effects=True, vmem_limit_bytes=VMEM_LIMIT
        ),
        name="triangle_back",
    )(g, lmat, rmat)


def total_kernel(terms_ref, sum_ref, in_ref, own_ref, sem_a, sem_b):
    r, q = lax.axis_index("row"), lax.axis_index("col")
    rows = terms_ref.shape[1]
    entry_barrier()
    exchange_start(terms_ref, in_ref, by_channel, by_channel, sem_a)
    exchange_wait(terms_ref, in_ref, sem_a)
    own = lax.fori_loop(
        0, ND, lambda s, acc: acc + in_ref[s].astype(F32), jnp.zeros((rows, 128), F32)
    )
    own_ref[...] = own.astype(BF)
    mine = by_channel(r, q)

    def send(pr, pq):
        pltpu.make_async_remote_copy(
            src_ref=own_ref,
            dst_ref=sum_ref.at[mine],
            send_sem=sem_b.at[0],
            recv_sem=sem_b.at[1],
            device_id=(pr, pq),
            device_id_type=MESH,
        ).start()

    each_peer(send)
    pltpu.make_async_copy(own_ref, sum_ref.at[mine], sem_b.at[2]).start()
    exchange_wait_send(terms_ref, in_ref, sem_a)
    exchange_wait(in_ref, sum_ref, sem_b)
    exchange_wait_send(in_ref, sum_ref, sem_b)


def total(terms):
    return pl.pallas_call(
        total_kernel,
        out_shape=sds(terms.shape, BF),
        in_specs=vspec(1),
        out_specs=pl.BlockSpec(memory_space=pltpu.VMEM),
        scratch_shapes=[
            pltpu.VMEM(terms.shape, BF),
            pltpu.VMEM(terms.shape[1:], BF),
            pltpu.SemaphoreType.DMA((3,)),
            pltpu.SemaphoreType.DMA((3,)),
        ],
        compiler_params=pltpu.CompilerParams(
            collective_id=3, has_side_effects=True, vmem_limit_bytes=VMEM_LIMIT
        ),
        name="total",
    )(terms)


def on_device(
    pair_act, cotangent, residue_mask, pair_mask, proj_weight, gate_weight, out_weight,
    trans_in, trans_out, norm_gains,
):
    live_res = residue_mask.astype(F32)
    row_live = lax.dynamic_slice_in_dim(live_res, lax.axis_index("row") * TI, TI)
    col_live = lax.dynamic_slice_in_dim(live_res, lax.axis_index("col") * TK, TK)
    live = pair_mask.astype(F32) * row_live[:, None] * col_live[None, :]
    live = jnp.pad(live.reshape(1, E), ((0, 7), (0, EP - E)))
    gains = jnp.pad(norm_gains.T, ((0, 0), (0, 125)))
    x = pair_act.reshape(E, C)
    cot = cotangent.reshape(E, C)
    proj_t = proj_weight.T
    lr = project(x, live, proj_t, gains)
    mix, lmat, rmat = triangle(lr)
    g, after, logit, mid = middle(
        x, cot, mix, gate_weight.T, out_weight, out_weight.T, trans_in, trans_in.T, trans_out, gains
    )
    back = triangle_back(g, lmat, rmat)
    weights = jnp.concatenate([proj_weight, gate_weight], axis=1)
    grad_pair, tail = last(x, live, back, logit, after, proj_t, weights, gains)
    terms = jnp.concatenate([mid.reshape(ND, 16, 128), tail.reshape(ND, 16, 128)], axis=1)
    sums = total(terms).astype(F32) / (TI * NR)
    mid = sums[:, :16].reshape(ND * 16, 128)
    tail = sums[:, 16:].reshape(ND * 16, 128)
    H = trans_out.shape[0]
    tin = mid[: 2 * H].reshape(2 * H // C, C, C).transpose(1, 0, 2).reshape(C, 2 * H)
    tout = mid[2 * H : 3 * H]
    ow = mid[3 * H : 3 * H + C]
    gw = mid[3 * H + C : 3 * H + 2 * C]
    pw = tail[: 4 * C].reshape(4, C, C).transpose(1, 0, 2).reshape(C, 4 * C)
    gains_out = jnp.concatenate([tail[4 * C : 4 * C + 1], mid[3 * H + 2 * C : 3 * H + 2 * C + 2]])
    return grad_pair.reshape(TI, TK, C), pw, gw, ow, tin, tout, gains_out


def solution(mesh):
    split = P("row", "col", None)
    in_specs = (split, split, P(), P("row", "col"), P(), P(), P(), P(), P(), P())
    out_specs = (split, P(), P(), P(), P(), P(), P())
    return jax.shard_map(
        on_device, mesh=mesh, in_specs=in_specs, out_specs=out_specs, check_vma=False
    )
```

time: 687 us -> 217 us (0.32)
  waiting for transfers between devices: 428 us -> 0 us
  Pallas kernels: 0 us -> 200 us
  blocking collectives: 68 us -> 0 us
  matrix products: 67.1 us -> 0 us
  local copies, waits for them, and re-layouts: 70.8 us -> 9.46 us
  other arithmetic: 36.3 us -> 6.36 us
  between operations: 14.4 us -> 0.73 us
    pallas_call x0 -> x6, Pallas kernels: none -> 200 us  [the longest x1 60.4 us: triangle(): pl.pallas_call(triangle_kernel, out_shape=(sds((C, MX_T, 128), BF), sds((...]
    all_gather x2 -> x0, waiting for transfers between devices: 144 us -> none  [the longest x1 79.5 us: on_device(): grad_row = lax.all_gather(grad_tile, 'col', axis=1, tiled=True)]
    reduce_scatter x2 -> x0, waiting for transfers between devices: 142 us -> none  [the longest x1 96 us: on_device(): lax.psum_scatter(partial_value.astype(jnp.bfloat16), 'col', scatter_dimen...]
    psum x1 -> x0, waiting for transfers between devices: 142 us -> none  [on_device(): lax.psum((grad_projw, grad_gatew, grad_outw, grad_tin, grad_tout, jnp.sta...]
    psum x1 -> x0, blocking collectives: 68 us -> none  [on_device(): lax.psum((grad_projw, grad_gatew, grad_outw, grad_tin, grad_tout, jnp.sta...]
    dot_general x17 -> x0, matrix products: 67.1 us -> none  [the longest x1 16 us: on_device(): jnp.einsum('ikc,jkc->ijc', left_tile, right_slab, preferred_element_type=...]
    all_gather x2 -> x0, local copies, waits for them, and re-layouts: 32.4 us -> none  [the longest x1 21.6 us: on_device(): right_slab = lax.all_gather(right_tile, 'row', axis=0, tiled=True)]
    convert_element_type x2 -> x0, local copies, waits for them, and re-layouts: 28.6 us -> none  [the longest x1 17.2 us: on_device(): jnp.einsum('ijc,ikc->jkc', grad_row, left_tile, preferred_element_type=jn...]
  transfers between devices with their start and end apart: 5 -> 0, of which waited for: 5 -> 0; matrix products, arithmetic and copies ran while one was open for 5% -> 0% of each run, Pallas kernels for 0% -> 0%
where the time goes in v1:
time: 217 us; the launch traced here: 216 us
  Pallas kernels  200 us (92%)
  local copies, waits for them, and re-layouts  9.46 us (4%)
  other arithmetic  6.36 us (3%)
    pallas_call x1, Pallas kernels, triangle(): pl.pallas_call(triangle_kernel, out_shape=(sds((C, MX_T, 128), BF), sds((...  60.4 us
    pallas_call x1, Pallas kernels, triangle_back(): pl.pallas_call(triangle_back_kernel, out_shape=sds((C, LR_T, 128), BF), i...  58.1 us
    pallas_call x1, Pallas kernels, total(): pl.pallas_call(total_kernel, out_shape=sds(terms.shape, BF), in_specs=vsp...  39.1 us
    pallas_call x1, Pallas kernels, middle(): pl.pallas_call(middle_kernel, out_shape=(sds((C, MX_T, 128), BF), sds((C,...  21.2 us
    pallas_call x1, Pallas kernels, last(): pl.pallas_call(last_kernel, out_shape=(sds((E, C), BF), sds((ND * 16, 128...  11 us
    pallas_call x1, Pallas kernels, project(): pl.pallas_call(project_kernel, out_shape=sds((C, LR_T, 128), BF), in_spec...  10 us
    unnamed x15, local copies, waits for them, and re-layouts  4.75 us

profile of v1, /device:TPU:1, one launch (start us, length us, event | category | flops | bytes accessed | tf_op | source)
XLA Modules:
  0.0 216.5 jit_solution(18104092079533743119)
XLA Ops:
  0.6 0.7 convert_element_type.14
  1.5 0.8 multiply_multiply_fusion
  2.4 0.6 pad.8.live_ref
  3.0 0.8 copy.18
  3.8 0.6 pad.9.gain_ref
  4.5 1.7 copy.17
  6.1 10.0 %project.1.lr_ref = bf16[128,48,128]{2,1,0:T(8,128)(2,1)} custom-call(bf16[2592,128]{1,0:T(8,128)(2,1)} %bitcast.29, f32[8,2688]{1,0:T(8,128)} %pad.8.live_ref, bf16[512,128]{1,0:T(8,128)(2,1)} %bitcast.33, f32[128,128]{1,0:T(8,128)} %pad.9.gain_ref), custom_call_target="tpu_custom_call" | custom-call | tf_op jit(solution)/shard_map/project/pallas_call | solution.py:114
  16.2 60.4 %triangle.1 = (bf16[128,32,128]{2,1,0:T(8,128)(2,1)}, bf16[576,1024]{1,0:T(8,128)(2,1)}, bf16[1024,1024]{1,0:T(8,128)(2,1)}) custom-call(bf16[128,48,128]{2,1,0:T(8,128)(2,1)} %project.1.lr_ref), custom_call_target="tpu_custom_call" | custom-call | tf_op jit(solution)/shard_map/triangle/pallas_call | solution.py:480
  76.6 0.8 copy.21
  77.4 0.7 copy.19
  78.2 0.7 copy.20
  78.9 21.2 %middle.1 = (bf16[128,32,128]{2,1,0:T(8,128)(2,1)}, f32[128,2688]{1,0:T(8,128)}, bf16[128,2688]{1,0:T(8,128)(2,1)}, bf16[2048,128]{1,0:T(8,128)(2,1)}) custom-call(bf16[2592,128]{1,0:T(8,128)(2,1)} %bitcast.30, bf16[2592,128]{1,0:T(8,128)(2,1)} %bitcast.39, bf16[128,32,128]{2,1,0:T(8,128)(2,1)} %get-tuple-element.16.mix_ref, bf16[128,128]{1,0:T(8,128)(2,1)} %bitcast.46, ...), custom_call_target="tpu_custom_call" | custom-call | tf_op jit(solution)/shard_map/middle/pallas_call | solution.py:217
  100.1 58.1 %triangle_back.1.back_ref = bf16[128,48,128]{2,1,0:T(8,128)(2,1)} custom-call(bf16[128,32,128]{2,1,0:T(8,128)(2,1)} %get-tuple-element.17.g_ref, bf16[576,1024]{1,0:T(8,128)(2,1)} %get-tuple-element.18.l_ref, bf16[1024,1024]{1,0:T(8,128)(2,1)} %get-tuple-element.19.r_ref), custom_call_target="tpu_custom_call" | custom-call | tf_op jit(solution)/shard_map/triangle_back/pallas_call | solution.py:550
  158.2 0.7 pad_maximum_fusion.1.w_ref
  158.9 11.0 %last.1 = (bf16[2592,128]{1,0:T(8,128)(2,1)}, bf16[2048,128]{1,0:T(8,128)(2,1)}) custom-call(bf16[2592,128]{1,0:T(8,128)(2,1)} %bitcast.31, f32[8,2688]{1,0:T(8,128)} %pad.8.live_ref, bf16[128,48,128]{2,1,0:T(8,128)(2,1)} %triangle_back.1.back_ref, bf16[128,2688]{1,0:T(8,128)(2,1)} %get-tuple-element.20.logit_ref, f32[128,2688]{1,0:T(8,128)} %get-tuple-element.21.after_ref, ...), custom_call_target="tpu_custom_call" | custom-call | tf_op jit(solution)/shard_map/last/pallas_call | solution.py:296
  170.0 2.1 pad_maximum_fusion.terms_ref
  172.1 39.1 %total.1 = bf16[128,32,128]{2,1,0:T(8,128)(2,1)} custom-call(bf16[128,32,128]{2,1,0:T(8,128)(2,1)} %pad_maximum_fusion.terms_ref), custom_call_target="tpu_custom_call" | custom-call | tf_op jit(solution)/shard_map/total/pallas_call | solution.py:602
  211.1 1.5 convert_multiply_fusion
  212.7 0.2 fusion
  212.9 0.6 pad_maximum_fusion.2
  213.5 0.8 copy.28
  214.3 0.7 fusion.1
  215.1 0.7 copy.29
  215.8 0.7 fusion.2
  (16 shorter events, 0.3 us)
Async XLA Ops:
  6.1 70.5 %copy-start = (bf16[128,1024]{1,0:T(8,128)(2,1)S(1)}, bf16[128,1024]{1,0:T(8,128)(2,1)}, u32[]{:S(2)}) copy-start(bf16[128,1024]{1,0:T(8,128)(2,1)} %ti_ref.1) | copy-start | bytes 786436
  6.1 71.3 %copy-start.4 = (bf16[128,128]{1,0:T(8,128)(2,1)S(1)}, bf16[128,128]{1,0:T(8,128)(2,1)}, u32[]{:S(2)}) copy-start(bf16[128,128]{1,0:T(8,128)(2,1)} %param.15) | copy-start | bytes 98308
  6.1 72.0 %copy-start.3 = (bf16[128,128]{1,0:T(8,128)(2,1)S(1)}, bf16[128,128]{1,0:T(8,128)(2,1)}, u32[]{:S(2)}) copy-start(bf16[128,128]{1,0:T(8,128)(2,1)} %wo_ref.1) | copy-start | bytes 98308
  100.1 58.2 %copy-start.1 = (bf16[128,512]{1,0:T(8,128)(2,1)S(1)}, bf16[128,512]{1,0:T(8,128)(2,1)}, u32[]{:S(2)}) copy-start(bf16[128,512]{1,0:T(8,128)(2,1)} %param.14) | copy-start | bytes 393220
  158.9 11.0 %copy-start.2 = (bf16[2048,128]{1,0:T(8,128)(2,1)S(1)}, bf16[2048,128]{1,0:T(8,128)(2,1)}, u32[]{:S(2)}) copy-start(bf16[2048,128]{1,0:T(8,128)(2,1)} %get-tuple-element.23) | copy-start | bytes 1572868

commit v2 on v0

v2 whole, which is shorter than its diff:
```python
import functools

import jax
import jax.numpy as jnp
from jax import lax
from jax.experimental import pallas as pl
from jax.experimental.pallas import tpu as pltpu
from jax.sharding import PartitionSpec as P

EPSILON = 1e-05
BF = jnp.bfloat16
F32 = jnp.float32
MESH = pl.DeviceIdType.MESH
C = 128
NR, NQ = 16, 8
ND = NR * NQ
TI, TK = 36, 72
E = TI * TK
NT = 21
EP = NT * 128
MROWS = TI * NR
KP = NQ * 128
CH = 384
MSG = 16
BLK = (MSG, 128)
A_TILES = 9
A_ROWS = 16
THIRD = 7
OWNERS = 33
VMEM_LIMIT = 60 * 2**20


def vspec(n):
    return [pl.BlockSpec(memory_space=pltpu.VMEM)] * n


def sds(shape, dtype):
    return jax.ShapeDtypeStruct(shape, dtype)


def sigmoid(v):
    return 0.5 * jnp.tanh(0.5 * v) + 0.5


def norm(v):
    center = v - jnp.mean(v, axis=0, keepdims=True)
    inverse = lax.rsqrt(jnp.mean(center * center, axis=0, keepdims=True) + EPSILON)
    return center * inverse, inverse


def norm_back(h, n, inverse):
    first = jnp.mean(h, axis=0, keepdims=True)
    second = jnp.mean(h * n, axis=0, keepdims=True)
    return inverse * (h - first - n * second)


def mm(a, b):
    return jnp.dot(a, b, preferred_element_type=F32)


def mm_nt(a, b):
    return lax.dot_general(a, b, (((1,), (1,)), ((), ())), preferred_element_type=F32)


def eye():
    return (
        lax.broadcasted_iota(jnp.int32, (C, C), 0) == lax.broadcasted_iota(jnp.int32, (C, C), 1)
    ).astype(BF)


def each_peer(fn):
    r, q = lax.axis_index("row"), lax.axis_index("col")

    def one(pr, dq):
        fn(pr, lax.rem(q + dq, NQ))

    for dq in range(1, NQ):
        one(r, dq)

    def body(dr, carry):
        pr = lax.rem(r + dr, NR)
        for dq in range(NQ):
            one(pr, dq)
        return carry

    lax.fori_loop(1, NR, body, 0)


def exchange_start(src, dst, src_slot, dst_slot, sems):
    r, q = lax.axis_index("row"), lax.axis_index("col")
    mine = dst_slot(r, q)

    def send(pr, pq):
        pltpu.make_async_remote_copy(
            src_ref=src.at[src_slot(pr, pq)],
            dst_ref=dst.at[mine],
            send_sem=sems.at[0],
            recv_sem=sems.at[1],
            device_id=(pr, pq),
            device_id_type=MESH,
        ).start()

    each_peer(send)
    pltpu.make_async_copy(src.at[src_slot(r, q)], dst.at[mine], sems.at[2]).start()


def exchange_wait(src, dst, sems):
    part = pl.ds(0, ND - 1)
    pltpu.make_async_copy(src.at[part], dst.at[part], sems.at[1]).wait()
    pltpu.make_async_copy(src.at[0], dst.at[0], sems.at[2]).wait()


def exchange_wait_send(src, dst, sems):
    part = pl.ds(0, ND - 1)
    pltpu.make_async_copy(src.at[part], dst.at[part], sems.at[0]).wait()


def by_channel(r, q):
    return r * NQ + q


def by_entry(r, q):
    return q * NR + r


def chunks(count, fn):
    def loop(i, carry):
        fn(i)
        return carry

    lax.fori_loop(0, count, loop, 0)


def widen(src, f_ref, base=0):
    def some(i):
        f_ref[pl.ds(pl.multiple_of(base + i * 256, 256), 256), :] = (
            src[pl.ds(i * 16, 16)].reshape(256, 128).astype(F32)
        )

    chunks(ND // 16, some)


def narrow(f_ref, dst):
    def some(i):
        dst[pl.ds(i * 16, 16)] = (
            f_ref[pl.ds(pl.multiple_of(i * 256, 256), 256), :].astype(BF).reshape(16, MSG, 128)
        )

    chunks(ND // 16, some)


def lane_iota():
    return lax.broadcasted_iota(jnp.int32, (8, 128), 1)


def roll(v, shift):
    shift %= 128
    return v if shift == 0 else pltpu.roll(v, shift, 1)


def split_rows(tile, rows):
    lane = lane_iota()
    tiles = {}

    def get(t):
        if t not in tiles:
            tiles[t] = tile(t)
        return tiles[t]

    out = []
    for ii in rows:
        t, l = divmod(TK * ii, 128)
        v = get(t)
        if l + TK > 128:
            v = jnp.where(lane >= l, v, get(t + 1))
        out.append((ii, jnp.where(lane < TK, roll(v, -l), 0.0)))
    return out


def join_rows(row, tiles):
    lane = lane_iota()
    rolled = {}
    out = []
    for t in tiles:
        first = (128 * t) // TK
        final = min((128 * t + 127) // TK, TI - 1)
        value = jnp.zeros((8, 128), F32)
        for ii in range(final, first - 1, -1):
            start = TK * ii - 128 * t
            if ii not in rolled:
                rolled[ii] = roll(row(ii), start)
            if ii == final and start + TK >= 128:
                value = rolled[ii]
            else:
                value = jnp.where(lane < start + TK, rolled[ii], value)
        out.append((t, value))
    return out


def put16(ref, ii, lanes, low, high):
    ref[ii * NR : (ii + 1) * NR, lanes] = jnp.concatenate([low, high], axis=0).astype(BF)


def q_lanes(q):
    return pl.ds(pl.multiple_of(q * 128, 128), 128)


def gather_tile(f_ref, base):
    return jnp.concatenate(
        [f_ref[pl.ds(base + 8 * g * MSG, 8, stride=MSG), :] for g in range(C // 8)], axis=0
    )


def sum_blocks(ref):
    def some(i, acc):
        for k in range(8):
            acc = acc + ref[i * 8 + k].astype(F32)
        return acc

    return lax.fori_loop(0, ND // 8, some, jnp.zeros(BLK, F32))


def third_steps(p):
    return ((p * THIRD, 0, 4), (p * THIRD + 4, 4, 3))


def block_kernel(
    x_ref, cot_ref, live_ref, pw_ref, gw_ref, ow_ref, ti_ref, to_ref, gain_ref,
    pair_o, pw_o, gw_o, ow_o, ti_o, to_o, gn_o,
    pwt, gwt, owt, tit, gcol, xt_ref, cott_ref, scaled_ref, proj_ref, gate_ref, gi_ref,
    after_ref, logit_ref, f_ref, fw_ref, l_ref, r_ref, rf_ref, m_ref, mt_ref, c1_ref,
    hid_ref, inner_ref, gh_ref, gp_ref, tin_acc, tout_acc, ow_acc, gw_acc, pw_acc, gn_acc,
    s_a, r_a, s_m, r_m, s_g, r_g, s_b, r_b, s_mid, r_mid, mid_own, mid_sum,
    s_tail, r_tail, tail_own, tail_sum,
    sem_a, sem_m, sem_g, sem_b, sem_mid, sem_mid2, sem_tail, sem_tail2,
):
    H = to_ref.shape[0]
    r, q = lax.axis_index("row"), lax.axis_index("col")
    me = by_channel(r, q)

    barrier = pltpu.get_barrier_semaphore()
    each_peer(
        lambda pr, pq: pl.semaphore_signal(barrier, inc=1, device_id=(pr, pq), device_id_type=MESH)
    )

    def flip(src, dst):
        for b in range(src.shape[1] // C):
            dst[b * C : (b + 1) * C, :] = src[:, b * C : (b + 1) * C].astype(F32).T.astype(BF)

    flip(pw_ref, pwt)
    flip(gw_ref, gwt)
    flip(ow_ref, owt)
    flip(ti_ref, tit)
    gcol[...] = jnp.concatenate([gain_ref[...], jnp.zeros((C - 3, C), F32)], axis=0).T
    gain_in, gain_out, gain_t = (lambda: gcol[:, 0:1]), (lambda: gcol[:, 1:2]), (lambda: gcol[:, 2:3])

    def load_t(ref, t0, nt):
        stop = min((t0 + nt) * 128, E)
        rows = ref[t0 * 128 : stop, :]
        pad = (t0 + nt) * 128 - stop
        if pad:
            rows = jnp.concatenate([rows, jnp.zeros((pad, C), rows.dtype)], axis=0)
        return mm_nt(eye(), rows)

    f_ref[2 * THIRD * C :, :] = jnp.zeros(((MSG - 2 * THIRD) * C, 128), F32)
    for p in range(3):
        for t0, slot, nt in third_steps(p):
            lanes = slice(t0 * 128, (t0 + nt) * 128)
            xt = load_t(x_ref, t0, nt)
            xt_ref[:, lanes] = xt.astype(BF)
            scaled = (norm(xt)[0] * gain_in()).astype(BF)
            scaled_ref[:, lanes] = scaled
            proj_ref[:, lanes] = mm(pwt[...], scaled)
            live = live_ref[0:1, lanes]
            for i in range(0, C, 8):
                left = sigmoid(proj_ref[i : i + 8, lanes]) * proj_ref[C + i : C + i + 8, lanes] * live
                right = (
                    sigmoid(proj_ref[2 * C + i : 2 * C + i + 8, lanes])
                    * proj_ref[3 * C + i : 3 * C + i + 8, lanes]
                    * live
                )
                for tt in range(nt):
                    f_ref[(slot + tt) * C + i : (slot + tt) * C + i + 8, :] = left[:, tt * 128 : tt * 128 + 128]
                    row = (THIRD + slot + tt) * C + i
                    f_ref[row : row + 8, :] = right[:, tt * 128 : tt * 128 + 128]

        def pick(i):
            for k in range(8):
                c = i * 8 + k
                s_a[p, c] = jnp.concatenate(
                    [f_ref[pl.ds(c, 8, stride=C), :], f_ref[pl.ds(8 * C + c, 8, stride=C), :]], axis=0
                ).astype(BF)

        chunks(C // 8, pick)
        if p == 0:
            pl.semaphore_wait(barrier, ND - 1)
        exchange_start(s_a.at[p], r_a.at[p], by_channel, by_entry, sem_a.at[p])

    for ref in (rf_ref, tin_acc, tout_acc, ow_acc, gw_acc, pw_acc, gn_acc):
        ref[...] = jnp.zeros_like(ref)
    for p in range(3):
        for t0, slot, nt in third_steps(p):
            lanes = slice(t0 * 128, (t0 + nt) * 128)
            cot_b = load_t(cot_ref, t0, nt).astype(BF)
            cott_ref[:, lanes] = cot_b
            gate_ref[:, lanes] = sigmoid(mm(gwt[...], scaled_ref[:, lanes]))
            gi_ref[:, lanes] = mm(to_ref[...], cot_b)

    for p in range(3):
        exchange_wait(s_a.at[p], r_a.at[p], sem_a.at[p])
        widen(r_a.at[p], fw_ref, p * ND * MSG)

        def per_col(qq):
            def tile(base, row0, stride):
                return lambda t: fw_ref[
                    pl.ds((t // THIRD) * ND * MSG + base * MSG + row0 + t % THIRD, 8, stride=stride), :
                ]

            rows = range(12 * p, 12 * p + 12)
            low = split_rows(tile(qq * NR, 0, MSG), rows)
            high = split_rows(tile(qq * NR + 8, 0, MSG), rows)
            for (ii, a), (_, b) in zip(low, high):
                put16(l_ref, ii, q_lanes(qq), a, b)
            for h in range(2):
                for jj, v in split_rows(tile(qq * NR + h, THIRD, 2 * MSG), rows):
                    rf_ref[pl.ds(qq * KP + h * TI + jj, 8, stride=128), :] = v
            if p == 2:
                r_ref[:, q_lanes(qq)] = rf_ref[pl.ds(pl.multiple_of(qq * KP, KP), KP), :].astype(BF)

        chunks(NQ, per_col)

    parts = ((0, 0, A_ROWS, 0, A_TILES), (1, A_ROWS, TI, A_TILES, NT))
    for part, i0, i1, t0, t1 in parts:
        rows = slice(i0 * NR, i1 * NR)
        for b in range(0, KP, 256):
            c1_ref[rows, b : b + 256] = mm_nt(l_ref[rows, :], r_ref[b : b + 256, :])

        def pack(qq):
            for h in range(2):
                row = lambda ii: c1_ref[ii * NR + 8 * h : ii * NR + 8 * h + 8, q_lanes(qq)]
                for t, v in join_rows(row, range(t0, t1)):
                    f_ref[pl.ds((qq * NR + 8 * h) * MSG + t - t0, 8, stride=MSG), :] = v

        chunks(NQ, pack)
        narrow(f_ref, s_m.at[part])
        exchange_start(s_m.at[part], r_m.at[part], by_entry, by_channel, sem_m.at[part])

    for part, i0, i1, t0, t1 in parts:
        exchange_wait(s_m.at[part], r_m.at[part], sem_m.at[part])
        widen(r_m.at[part], fw_ref)

        def step(k):
            lanes = pl.ds(pl.multiple_of(t0 * 128 + k * CH, 128), CH)
            mixed = jnp.concatenate([gather_tile(fw_ref, k * 3 + tt) for tt in range(3)], axis=1)
            normed_x, r_x = norm(mixed)
            scaled_out = (normed_x * gain_out()).astype(BF)
            output = mm(owt[...], scaled_out)
            gate = gate_ref[:, lanes]
            after = (xt_ref[:, lanes].astype(F32) + gate * output).astype(BF).astype(F32)
            normed_t, r_t = norm(after)
            scaled_t = (normed_t * gain_t()).astype(BF)
            hid_ref[...] = mm(tit[...], scaled_t)
            for i in range(0, H, 16):
                g = hid_ref[i : i + 16, :]
                u = hid_ref[H + i : H + i + 16, :]
                gi = gi_ref[i : i + 16, lanes]
                sg = sigmoid(g)
                swish = g * sg
                inner_ref[i : i + 16, :] = (swish * u).astype(BF)
                gh_ref[i : i + 16, :] = (gi * u * (sg + swish * (1.0 - sg))).astype(BF)
                gh_ref[H + i : H + i + 16, :] = (gi * swish).astype(BF)
            cot_b = cott_ref[:, lanes]
            back_t = mm(ti_ref[...], gh_ref[...])
            tout_acc[...] += mm_nt(inner_ref[...], cot_b)
            tin_acc[...] += mm_nt(gh_ref[...], scaled_t)
            gn_acc[1, :, :CH] += back_t * normed_t
            grad_after = cot_b.astype(F32) + norm_back(back_t * gain_t(), normed_t, r_t)
            after_ref[:, lanes] = grad_after
            grad_output = (grad_after * gate).astype(BF)
            grad_logit = (grad_after * output * gate * (1.0 - gate)).astype(BF)
            logit_ref[:, lanes] = grad_logit
            gw_acc[...] += mm_nt(scaled_ref[:, lanes], grad_logit)
            ow_acc[...] += mm_nt(scaled_out, grad_output)
            back_x = mm(ow_ref[...], grad_output)
            gn_acc[0, :, :CH] += back_x * normed_x
            grad_mixed = norm_back(back_x * gain_out(), normed_x, r_x)
            for tt in range(3):
                for g in range(C // 8):
                    f_ref[pl.ds(k * 3 + tt + 8 * g * MSG, 8, stride=MSG), :] = grad_mixed[
                        8 * g : 8 * g + 8, tt * 128 : (tt + 1) * 128
                    ]

        chunks((t1 - t0) // 3, step)
        narrow(f_ref, s_g.at[part])
        exchange_start(s_g.at[part], r_g.at[part], by_channel, by_entry, sem_g.at[part])

    def put_terms(dst, first, value):
        n = value.shape[0] // MSG
        dst[first // MSG : first // MSG + n] = value.astype(BF).reshape(n, MSG, 128)

    def gain_rows(values):
        rows = [jnp.sum(v.T, axis=0, keepdims=True) for v in values]
        return jnp.concatenate(rows + [jnp.zeros((MSG - len(rows), 128), F32)], axis=0)

    put_terms(s_mid, 0, tin_acc[...])
    put_terms(s_mid, 2 * H, tout_acc[...])
    put_terms(s_mid, 3 * H, ow_acc[...])
    put_terms(s_mid, 3 * H + C, gw_acc[...])
    rest = 3 * H + 2 * C
    put_terms(s_mid, rest, gain_rows([gn_acc[0], gn_acc[1]]))
    s_mid[rest // MSG + 1 :] = jnp.zeros((ND - rest // MSG - 1, MSG, 128), BF)
    exchange_start(s_mid, r_mid, by_channel, by_channel, sem_mid)

    for part, i0, i1, t0, t1 in parts:
        rows = slice(i0 * NR, i1 * NR)
        exchange_wait(s_g.at[part], r_g.at[part], sem_g.at[part])
        widen(r_g.at[part], fw_ref)

        def per_col(qq):
            def tile(h):
                return lambda t: fw_ref[pl.ds((qq * NR + 8 * h) * MSG + t - t0, 8, stride=MSG), :]

            low, high = split_rows(tile(0), range(i0, i1)), split_rows(tile(1), range(i0, i1))
            for (ii, a), (_, b) in zip(low, high):
                put16(m_ref, ii, q_lanes(qq), a, b)

        chunks(NQ, per_col)
        for b in range(0, KP, 256):
            c1_ref[rows, b : b + 256] = mm(m_ref[rows, :], r_ref[:, b : b + 256])
        for b in range(0, KP, 128):
            mt_ref[b : b + 128, rows] = mm_nt(eye(), m_ref[rows, b : b + 128]).astype(BF)
    for b in range(0, KP, 256):
        both = mm(mt_ref[...], l_ref[:, b : b + 256])
        rf_ref[b // 128 * KP : (b // 128 + 1) * KP, :] = both[:, :128]
        rf_ref[(b // 128 + 1) * KP : (b // 128 + 2) * KP, :] = both[:, 128:]

    for p in range(3):
        tiles = range(p * THIRD, (p + 1) * THIRD)

        def pack(qq):
            for h in range(2):
                row = lambda ii: c1_ref[ii * NR + 8 * h : ii * NR + 8 * h + 8, q_lanes(qq)]
                for t, v in join_rows(row, tiles):
                    f_ref[pl.ds((qq * NR + 8 * h) * MSG + t - p * THIRD, 8, stride=MSG), :] = v
                row = lambda jj: rf_ref[pl.ds(qq * KP + h * TI + jj, 8, stride=128), :]
                for t, v in join_rows(row, tiles):
                    f_ref[pl.ds((qq * NR + h) * MSG + THIRD + t - p * THIRD, 8, stride=2 * MSG), :] = v

        chunks(NQ, pack)
        narrow(f_ref, s_b.at[p])
        exchange_start(s_b.at[p], r_b.at[p], by_entry, by_channel, sem_b.at[p])

    def spread(own, dst, slot, sems):
        def send(pr, pq):
            pltpu.make_async_remote_copy(
                src_ref=own,
                dst_ref=dst.at[slot],
                send_sem=sems.at[0],
                recv_sem=sems.at[1],
                device_id=(pr, pq),
                device_id_type=MESH,
            ).start()

        each_peer(send)
        pltpu.make_async_copy(own, dst.at[slot], sems.at[2]).start()

    exchange_wait(s_mid, r_mid, sem_mid)
    mid_own[...] = sum_blocks(r_mid).astype(BF)
    spread(mid_own, mid_sum, me, sem_mid2)

    for p in range(3):
        exchange_wait(s_b.at[p], r_b.at[p], sem_b.at[p])
        widen(r_b.at[p], fw_ref)
        for t0, slot, nt in third_steps(p):
            w = nt * 128
            lanes = slice(t0 * 128, t0 * 128 + w)
            live = live_ref[0:1, lanes]
            for i in range(0, C, 16):
                def grads(base):
                    return live * jnp.concatenate(
                        [
                            jnp.concatenate(
                                [fw_ref[pl.ds(base + slot + tt + (i + 8 * g) * MSG, 8, stride=MSG), :] for g in range(2)],
                                axis=0,
                            )
                            for tt in range(nt)
                        ],
                        axis=1,
                    )

                for k, base in ((0, 0), (2, THIRD)):
                    grad = grads(base)
                    s = sigmoid(proj_ref[k * C + i : k * C + i + 16, lanes])
                    gs = grad * s
                    gp_ref[(k + 1) * C + i : (k + 1) * C + i + 16, :w] = gs.astype(BF)
                    gp_ref[k * C + i : k * C + i + 16, :w] = (
                        gs * proj_ref[(k + 1) * C + i : (k + 1) * C + i + 16, lanes] * (1.0 - s)
                    ).astype(BF)
            normed, inverse = norm(xt_ref[:, lanes].astype(F32))
            pw_acc[...] += mm_nt(gp_ref[:, :w], scaled_ref[:, lanes])
            back = mm(pw_ref[...], gp_ref[:, :w]) + mm(gw_ref[...], logit_ref[:, lanes])
            prod = back * normed
            gn_acc[2, :, :384] += prod[:, :384]
            if w > 384:
                gn_acc[2, :, 384:w] += prod[:, 384:]
            after_ref[:, lanes] += norm_back(back * gain_in(), normed, inverse)

    put_terms(s_tail, 0, pw_acc[...])
    put_terms(s_tail, 4 * C, gain_rows([gn_acc[2]]))
    even = lax.rem(r, 4) == 0
    odd_one = jnp.logical_and(r == 2, q == 0)
    owner = jnp.logical_or(even, odd_one)
    my_part = jnp.where(even, (r // 4) * NQ + q, OWNERS - 1)

    def tail_send(o, pr, pq):
        remote = jnp.logical_or(pr != r, pq != q)

        @pl.when(remote)
        def _():
            pltpu.make_async_remote_copy(
                src_ref=s_tail.at[o],
                dst_ref=r_tail.at[me],
                send_sem=sem_tail.at[0],
                recv_sem=sem_tail.at[1],
                device_id=(pr, pq),
                device_id_type=MESH,
            ).start()

        @pl.when(jnp.logical_not(remote))
        def _():
            pltpu.make_async_copy(s_tail.at[o], r_tail.at[me], sem_tail.at[2]).start()

    def four(i, carry):
        for k in range(NQ):
            tail_send(i * NQ + k, 4 * i, k)
        return carry

    lax.fori_loop(0, 4, four, 0)
    tail_send(OWNERS - 1, 2, 0)

    for t0 in range(0, NT, 3):
        stop = min((t0 + 3) * 128, E)
        pair_o[t0 * 128 : stop, :] = after_ref[:, t0 * 128 : t0 * 128 + 384].T[: stop - t0 * 128].astype(BF)

    @pl.when(owner)
    def _():
        exchange_wait(r_tail, r_tail, sem_tail)
        tail_own[...] = sum_blocks(r_tail).astype(BF)
        spread(tail_own, tail_sum, my_part, sem_tail2)

    scale = 1.0 / (TI * NR)

    def total(ref, first, rows):
        return ref[first // MSG : (first + rows) // MSG].reshape(rows, 128).astype(F32) * scale

    exchange_wait(r_mid, mid_sum, sem_mid2)
    for b in range(0, 2 * H, C):
        ti_o[:, b : b + C] = total(mid_sum, b, C).T
    to_o[...] = total(mid_sum, 2 * H, H)
    ow_o[...] = total(mid_sum, 3 * H, C)
    gw_o[...] = total(mid_sum, 3 * H + C, C)

    def tail_wait(n):
        pltpu.make_async_copy(r_tail.at[pl.ds(0, n)], r_tail.at[pl.ds(0, n)], sem_tail2.at[1]).wait()

    @pl.when(owner)
    def _():
        tail_wait(OWNERS - 1)
        pltpu.make_async_copy(tail_own, tail_sum.at[0], sem_tail2.at[2]).wait()

    @pl.when(jnp.logical_not(owner))
    def _():
        tail_wait(OWNERS)

    for b in range(0, 4 * C, C):
        pw_o[:, b : b + C] = total(tail_sum, b, C).T
    gn_o[...] = jnp.concatenate(
        [total(tail_sum, 4 * C, MSG)[0:1], total(mid_sum, rest, MSG)[0:2]], axis=0
    )

    for p in range(3):
        exchange_wait_send(s_a.at[p], r_a.at[p], sem_a.at[p])
        exchange_wait_send(s_b.at[p], r_b.at[p], sem_b.at[p])
    for part in range(2):
        exchange_wait_send(s_m.at[part], r_m.at[part], sem_m.at[part])
        exchange_wait_send(s_g.at[part], r_g.at[part], sem_g.at[part])
    exchange_wait_send(s_mid, r_mid, sem_mid)
    exchange_wait_send(r_mid, mid_sum, sem_mid2)

    def tail_left(n, sem):
        pltpu.make_async_copy(r_tail.at[pl.ds(0, n)], r_tail.at[pl.ds(0, n)], sem).wait()

    @pl.when(owner)
    def _():
        tail_left(OWNERS - 1, sem_tail.at[0])
        tail_left(ND - 1, sem_tail2.at[0])

    @pl.when(jnp.logical_not(owner))
    def _():
        tail_left(OWNERS, sem_tail.at[0])


def block(x, cot, live, pw, gw, ow, ti, to, gains):
    H = to.shape[0]
    msgs = lambda *lead: pltpu.VMEM((*lead, ND, MSG, 128), BF)
    dma = lambda *shape: pltpu.SemaphoreType.DMA(shape)
    v = pltpu.VMEM
    return pl.pallas_call(
        block_kernel,
        out_shape=(
            sds((E, C), BF), sds(pw.shape, F32), sds(gw.shape, F32), sds(ow.shape, F32),
            sds(ti.shape, F32), sds(to.shape, F32), sds(gains.shape, F32),
        ),
        in_specs=vspec(9),
        out_specs=tuple(vspec(7)),
        scratch_shapes=[
            v((4 * C, C), BF), v((C, C), BF), v((C, C), BF), v((2 * H, C), BF), v((C, C), F32),
            v((C, EP), BF), v((C, EP), BF), v((C, EP), BF), v((4 * C, EP), F32), v((C, EP), F32),
            v((H, EP), F32), v((C, EP), F32), v((C, EP), BF),
            v((ND * MSG, 128), F32), v((3 * ND * MSG, 128), F32),
            v((MROWS, KP), BF), v((KP, KP), BF), v((NQ * KP, 128), F32), v((MROWS, KP), BF),
            v((KP, MROWS), BF), v((MROWS, KP), F32),
            v((2 * H, CH), F32), v((H, CH), BF), v((2 * H, CH), BF), v((4 * C, 512), BF),
            v((2 * H, C), F32), v((H, C), F32), v((C, C), F32), v((C, C), F32), v((4 * C, C), F32),
            v((3, C, 512), F32),
            msgs(3), msgs(3), msgs(2), msgs(2), msgs(2), msgs(2), msgs(3), msgs(3), msgs(), msgs(),
            v(BLK, BF), msgs(),
            v((OWNERS, *BLK), BF), msgs(), v(BLK, BF), v((OWNERS, *BLK), BF),
            dma(3, 3), dma(2, 3), dma(2, 3), dma(3, 3), dma(3), dma(3), dma(3), dma(3),
        ],
        compiler_params=pltpu.CompilerParams(
            collective_id=1, has_side_effects=True, vmem_limit_bytes=VMEM_LIMIT
        ),
        name="block",
    )(x, cot, live, pw, gw, ow, ti, to, gains)


def on_device(
    pair_act, cotangent, residue_mask, pair_mask, proj_weight, gate_weight, out_weight,
    trans_in, trans_out, norm_gains,
):
    live_res = residue_mask.astype(F32)
    row_live = lax.dynamic_slice_in_dim(live_res, lax.axis_index("row") * TI, TI)
    col_live = lax.dynamic_slice_in_dim(live_res, lax.axis_index("col") * TK, TK)
    live = pair_mask.astype(F32) * row_live[:, None] * col_live[None, :]
    live = jnp.pad(live.reshape(1, E), ((0, 7), (0, EP - E)))
    out = block(
        pair_act.reshape(E, C), cotangent.reshape(E, C), live, proj_weight, gate_weight,
        out_weight, trans_in, trans_out, norm_gains,
    )
    return (out[0].reshape(TI, TK, C), *out[1:])


def solution(mesh):
    split = P("row", "col", None)
    in_specs = (split, split, P(), P("row", "col"), P(), P(), P(), P(), P(), P())
    out_specs = (split, P(), P(), P(), P(), P(), P())
    return jax.shard_map(
        on_device, mesh=mesh, in_specs=in_specs, out_specs=out_specs, check_vma=False
    )
```

time: 687 us -> 126 us (0.18)
  waiting for transfers between devices: 428 us -> 0 us
  Pallas kernels: 0 us -> 117 us
  blocking collectives: 68 us -> 0 us
  matrix products: 67.1 us -> 0 us
  local copies, waits for them, and re-layouts: 70.8 us -> 8.18 us
  other arithmetic: 36.3 us -> 0.08 us
  between operations: 14.4 us -> 0.69 us
    all_gather x2 -> x0, waiting for transfers between devices: 144 us -> none  [the longest x1 79.5 us: on_device(): grad_row = lax.all_gather(grad_tile, 'col', axis=1, tiled=True)]
    reduce_scatter x2 -> x0, waiting for transfers between devices: 142 us -> none  [the longest x1 96 us: on_device(): lax.psum_scatter(partial_value.astype(jnp.bfloat16), 'col', scatter_dimen...]
    psum x1 -> x0, waiting for transfers between devices: 142 us -> none  [on_device(): lax.psum((grad_projw, grad_gatew, grad_outw, grad_tin, grad_tout, jnp.sta...]
    pallas_call x0 -> x1, Pallas kernels: none -> 117 us  [block(): pl.pallas_call(block_kernel, out_shape=(sds((E, C), BF), sds(pw.shape, F3...]
    psum x1 -> x0, blocking collectives: 68 us -> none  [on_device(): lax.psum((grad_projw, grad_gatew, grad_outw, grad_tin, grad_tout, jnp.sta...]
    dot_general x17 -> x0, matrix products: 67.1 us -> none  [the longest x1 16 us: on_device(): jnp.einsum('ikc,jkc->ijc', left_tile, right_slab, preferred_element_type=...]
    all_gather x2 -> x0, local copies, waits for them, and re-layouts: 32.4 us -> none  [the longest x1 21.6 us: on_device(): right_slab = lax.all_gather(right_tile, 'row', axis=0, tiled=True)]
    convert_element_type x2 -> x0, local copies, waits for them, and re-layouts: 28.6 us -> none  [the longest x1 17.2 us: on_device(): jnp.einsum('ijc,ikc->jkc', grad_row, left_tile, preferred_element_type=jn...]
  transfers between devices with their start and end apart: 5 -> 0, of which waited for: 5 -> 0; matrix products, arithmetic and copies ran while one was open for 5% -> 0% of each run, Pallas kernels for 0% -> 0%
where the time goes in v2:
time: 126 us
  Pallas kernels  117 us (93%)
  local copies, waits for them, and re-layouts  8.18 us (6%)
    pallas_call x1, Pallas kernels, block(): pl.pallas_call(block_kernel, out_shape=(sds((E, C), BF), sds(pw.shape, F3...  117 us
    unnamed x23, local copies, waits for them, and re-layouts  7.29 us

profile of v2, /device:TPU:1, one launch (start us, length us, event | category | flops | bytes accessed | tf_op | source)
XLA Modules:
  0.0 125.7 jit_solution(2015056310541094393)
XLA Ops:
  0.6 0.0 copy-start.5
  0.6 0.0 copy-start.6
  0.7 0.7 copy-done.6
  1.3 0.1 dynamic_slice.7
  1.4 0.1 dynamic_slice.6
  1.5 0.0 copy-done.5
  1.5 0.1 multiply_multiply_fusion
  1.6 0.1 reshape.30
  1.7 0.6 pad.4.live_ref
  2.3 116.8 %block.1 = (bf16[2592,128]{1,0:T(8,128)(2,1)}, f32[128,512]{1,0:T(8,128)}, f32[128,128]{1,0:T(8,128)}, f32[128,128]{1,0:T(8,128)}, f32[128,1024]{1,0:T(8,128)}, /*index=5*/f32[512,128]{1,0:T(8,128)}, f32[3,128]{1,0:T(4,128)}) custom-call(bf16[2592,128]{1,0:T(8,128)(2,1)} %bitcast.3, bf16[2592,128]{1,0:T(8,128)(2,1)} %bitcast.4, f32[8,2688]{1,0:T(8,128)} %pad.4.live_ref, ...), custom_call_target="tpu_custom_call" | custom-call | tf_op jit(solution)/shard_map/block/pallas_call | solution.py:608
  119.1 0.0 copy-start.2
  119.1 0.0 copy-start.4
  119.1 2.0 %copy.24 = bf16[36,72,128]{2,1,0:T(8,128)(2,1)} copy(bf16[36,72,128]{2,1,0:T(8,128)(2,1)} %bitcast.5) | data formatting | bytes 1327104
  121.1 0.0 copy-done.2
  121.2 0.7 copy.25
  121.9 0.0 copy-done.4
  121.9 0.6 copy.26
  122.5 0.2 copy-done.3
  122.7 0.6 copy.27
  123.4 0.8 copy.28
  124.1 0.3 copy-done.1
  124.4 0.7 copy.29
  125.1 0.0 copy-done.7
  125.2 0.6 copy.30
  (6 shorter events, 0.0 us)
Async XLA Ops:
  0.6 0.9 copy-start.5
  0.6 0.7 copy-start.6
  119.1 2.0 %copy-start.2 = (f32[128,512]{1,0:T(8,128)S(1)}, f32[128,512]{1,0:T(8,128)}, u32[]{:S(2)}) copy-start(f32[128,512]{1,0:T(8,128)} %get-tuple-element.29) | copy-start | bytes 786436
  119.1 2.7 %copy-start.4 = (f32[128,128]{1,0:T(8,128)S(1)}, f32[128,128]{1,0:T(8,128)}, u32[]{:S(2)}) copy-start(f32[128,128]{1,0:T(8,128)} %get-tuple-element.30) | copy-start | bytes 196612
  121.1 2.2 %copy-start = (f32[128,1024]{1,0:T(8,128)S(1)}, f32[128,1024]{1,0:T(8,128)}, u32[]{:S(2)}) copy-start(f32[128,1024]{1,0:T(8,128)} %get-tuple-element.32) | copy-start | bytes 1572868
  121.9 0.9 copy-start.3
  123.4 1.1 copy-start.1
  124.4 0.7 copy-start.7

commit v3 on v2

v3 whole, which is shorter than its diff:
```python
import functools

import jax
import jax.numpy as jnp
from jax import lax
from jax.experimental import pallas as pl
from jax.experimental.pallas import tpu as pltpu
from jax.sharding import PartitionSpec as P

EPSILON = 1e-05
BF = jnp.bfloat16
F32 = jnp.float32
MESH = pl.DeviceIdType.MESH
C = 128
NR, NQ = 16, 8
ND = NR * NQ
TI, TK = 36, 72
E = TI * TK
NT = 21
EP = NT * 128
MROWS = TI * NR
KP = NQ * 128
MSG = 16
BLK = (MSG, 128)
G_TILES, G_ROWS = 13, 23
A_ROWS = 16
THIRD = 7
OWNERS = 33
VMEM_LIMIT = 60 * 2**20


def vspec(n):
    return [pl.BlockSpec(memory_space=pltpu.VMEM)] * n


def sds(shape, dtype):
    return jax.ShapeDtypeStruct(shape, dtype)


def sigmoid(v):
    return 0.5 * jnp.tanh(0.5 * v) + 0.5


def norm(v):
    center = v - jnp.mean(v, axis=0, keepdims=True)
    inverse = lax.rsqrt(jnp.mean(center * center, axis=0, keepdims=True) + EPSILON)
    return center * inverse, inverse


def norm_back(h, n, inverse):
    first = jnp.mean(h, axis=0, keepdims=True)
    second = jnp.mean(h * n, axis=0, keepdims=True)
    return inverse * (h - first - n * second)


def mm(a, b):
    return jnp.dot(a, b, preferred_element_type=F32)


def mm_nt(a, b):
    return lax.dot_general(a, b, (((1,), (1,)), ((), ())), preferred_element_type=F32)


def eye():
    return (
        lax.broadcasted_iota(jnp.int32, (C, C), 0) == lax.broadcasted_iota(jnp.int32, (C, C), 1)
    ).astype(BF)


def each_peer(fn):
    r, q = lax.axis_index("row"), lax.axis_index("col")

    def one(pr, dq):
        fn(pr, lax.rem(q + dq, NQ))

    for dq in range(1, NQ):
        one(r, dq)

    def body(dr, carry):
        pr = lax.rem(r + dr, NR)
        for dq in range(NQ):
            one(pr, dq)
        return carry

    lax.fori_loop(1, NR, body, 0)


def exchange_start(src, dst, src_slot, dst_slot, sems):
    r, q = lax.axis_index("row"), lax.axis_index("col")
    mine = dst_slot(r, q)

    def send(pr, pq):
        pltpu.make_async_remote_copy(
            src_ref=src.at[src_slot(pr, pq)],
            dst_ref=dst.at[mine],
            send_sem=sems.at[0],
            recv_sem=sems.at[1],
            device_id=(pr, pq),
            device_id_type=MESH,
        ).start()

    each_peer(send)
    pltpu.make_async_copy(src.at[src_slot(r, q)], dst.at[mine], sems.at[2]).start()


def exchange_wait(src, dst, sems):
    part = pl.ds(0, ND - 1)
    pltpu.make_async_copy(src.at[part], dst.at[part], sems.at[1]).wait()
    pltpu.make_async_copy(src.at[0], dst.at[0], sems.at[2]).wait()


def exchange_wait_send(src, dst, sems):
    part = pl.ds(0, ND - 1)
    pltpu.make_async_copy(src.at[part], dst.at[part], sems.at[0]).wait()


def by_channel(r, q):
    return r * NQ + q


def by_entry(r, q):
    return q * NR + r


def chunks(count, fn):
    def loop(i, carry):
        fn(i)
        return carry

    lax.fori_loop(0, count, loop, 0)


def widen(src, f_ref, base=0):
    rows = src.shape[1]

    def some(i):
        f_ref[pl.ds(pl.multiple_of(base + i * 16 * rows, 128), 16 * rows), :] = (
            src[pl.ds(i * 16, 16)].astype(F32).reshape(16 * rows, 128)
        )

    chunks(ND // 16, some)


def narrow(f_ref, dst):
    rows = dst.shape[1]

    def some(i):
        dst[pl.ds(i * 16, 16)] = (
            f_ref[pl.ds(pl.multiple_of(i * 16 * rows, 128), 16 * rows), :].reshape(16, rows, 128).astype(BF)
        )

    chunks(ND // 16, some)


def lane_iota():
    return lax.broadcasted_iota(jnp.int32, (8, 128), 1)


def roll(v, shift):
    shift %= 128
    return v if shift == 0 else pltpu.roll(v, shift, 1)


def split_rows(tile, rows):
    lane = lane_iota()
    tiles = {}

    def get(t):
        if t not in tiles:
            tiles[t] = tile(t)
        return tiles[t]

    out = []
    for ii in rows:
        t, l = divmod(TK * ii, 128)
        v = get(t)
        if l + TK > 128:
            v = jnp.where(lane >= l, v, get(t + 1))
        out.append((ii, jnp.where(lane < TK, roll(v, -l), 0.0)))
    return out


def join_rows(row, tiles):
    lane = lane_iota()
    rolled = {}
    out = []
    for t in tiles:
        first = (128 * t) // TK
        final = min((128 * t + 127) // TK, TI - 1)
        value = jnp.zeros((8, 128), F32)
        for ii in range(final, first - 1, -1):
            start = TK * ii - 128 * t
            if ii not in rolled:
                rolled[ii] = roll(row(ii), start)
            if ii == final and start + TK >= 128:
                value = rolled[ii]
            else:
                value = jnp.where(lane < start + TK, rolled[ii], value)
        out.append((t, value))
    return out


def put16(ref, ii, lanes, low, high):
    ref[ii * NR : (ii + 1) * NR, lanes] = jnp.concatenate([low, high], axis=0).astype(BF)


def q_lanes(q):
    return pl.ds(pl.multiple_of(q * 128, 128), 128)


def fold(v):
    return sum(v[:, k : k + 128] for k in range(128, v.shape[1], 128)) + v[:, :128]


def sum_blocks(ref):
    def some(i, acc):
        for k in range(8):
            acc = acc + ref[i * 8 + k].astype(F32)
        return acc

    return lax.fori_loop(0, ND // 8, some, jnp.zeros(BLK, F32))


def block_kernel(
    x_ref, cot_ref, live_ref, pw_ref, gw_ref, ow_ref, ti_ref, to_ref, gain_ref,
    pair_o, mid_sum, tail_sum,
    pwt, gwt, owt, tit, gcol, xt_ref, cott_ref, scaled_ref, proj_ref, gate_ref,
    after_ref, logit_ref, f_ref, fw_ref, l_ref, r_ref, rf_ref, m_ref, mt_ref, c1_ref,
    hid_ref, gi_ref, inner_ref, gh_ref, gp_ref, tin_acc, tout_acc, ow_acc, gw_acc, pw_acc, gn_acc,
    s_a, r_a, s_m0, r_m0, s_m1, r_m1, s_g0, r_g0, s_g1, r_g1, s_b2, r_b2, s_b3, r_b3,
    s_mid, r_mid, mid_own,
    s_tail, r_tail, tail_own,
    sem_a, sem_m, sem_g, sem_b, sem_mid, sem_mid2, sem_tail, sem_tail2, entered,
):
    H = to_ref.shape[0]
    r, q = lax.axis_index("row"), lax.axis_index("col")
    me = by_channel(r, q)

    barrier = pltpu.get_barrier_semaphore()

    def greet(sem, pr, pq):
        pl.semaphore_signal(sem, inc=1, device_id=(pr, pq), device_id_type=MESH)

    for d in range(1, NQ):
        greet(barrier, r, lax.rem(q + d, NQ))
    for d in range(1, NR):
        greet(barrier, lax.rem(r + d, NR), q)

    def flip(src, dst):
        for b in range(src.shape[1] // C):
            dst[b * C : (b + 1) * C, :] = src[:, b * C : (b + 1) * C].astype(F32).T.astype(BF)

    flip(pw_ref, pwt)
    gcol[...] = jnp.concatenate([gain_ref[...], jnp.zeros((C - 3, C), F32)], axis=0).T
    gain_in, gain_out, gain_t = (lambda: gcol[:, 0:1]), (lambda: gcol[:, 1:2]), (lambda: gcol[:, 2:3])

    def load_t(ref, t0, nt):
        stop = min((t0 + nt) * 128, E)
        rows = ref[t0 * 128 : stop, :]
        pad = (t0 + nt) * 128 - stop
        if pad:
            rows = jnp.concatenate([rows, jnp.zeros((pad, C), rows.dtype)], axis=0)
        return mm_nt(eye(), rows)

    pl.semaphore_wait(barrier, NR + NQ - 2)
    for d in range(1, NQ):
        greet(entered, r, lax.rem(q + d, NQ))

    f_ref[2 * THIRD * C :, :] = jnp.zeros(((MSG - 2 * THIRD) * C, 128), F32)
    for p in range(3):
        for t0, slot, nt in ((p * THIRD, 0, THIRD),):
            lanes = slice(t0 * 128, (t0 + nt) * 128)
            xt = load_t(x_ref, t0, nt)
            xt_ref[:, lanes] = xt.astype(BF)
            scaled = (norm(xt)[0] * gain_in()).astype(BF)
            scaled_ref[:, lanes] = scaled
            proj_ref[:, lanes] = mm(pwt[...], scaled)
            live = live_ref[0:1, lanes]
            for i in range(0, C, 8):
                left = sigmoid(proj_ref[i : i + 8, lanes]) * proj_ref[C + i : C + i + 8, lanes] * live
                right = (
                    sigmoid(proj_ref[2 * C + i : 2 * C + i + 8, lanes])
                    * proj_ref[3 * C + i : 3 * C + i + 8, lanes]
                    * live
                )
                for tt in range(nt):
                    f_ref[(slot + tt) * C + i : (slot + tt) * C + i + 8, :] = left[:, tt * 128 : tt * 128 + 128]
                    row = (THIRD + slot + tt) * C + i
                    f_ref[row : row + 8, :] = right[:, tt * 128 : tt * 128 + 128]

        def pick(i):
            for k in range(8):
                c = i * 8 + k
                s_a[p, c] = jnp.concatenate(
                    [f_ref[pl.ds(c, 8, stride=C), :], f_ref[pl.ds(8 * C + c, 8, stride=C), :]], axis=0
                ).astype(BF)

        chunks(C // 8, pick)
        if p == 0:
            pl.semaphore_wait(entered, NQ - 1)
        exchange_start(s_a.at[p], r_a.at[p], by_channel, by_entry, sem_a.at[p])

    flip(gw_ref, gwt)
    flip(ow_ref, owt)
    flip(ti_ref, tit)
    for ref in (rf_ref, tin_acc, tout_acc, ow_acc, gw_acc, pw_acc, gn_acc):
        ref[...] = jnp.zeros_like(ref)
    for t0 in range(0, NT, THIRD):
        lanes = slice(t0 * 128, (t0 + THIRD) * 128)
        cott_ref[:, lanes] = load_t(cot_ref, t0, THIRD).astype(BF)
        gate_ref[:, lanes] = sigmoid(mm(gwt[...], scaled_ref[:, lanes]))

    for p in range(3):
        exchange_wait(s_a.at[p], r_a.at[p], sem_a.at[p])
        widen(r_a.at[p], fw_ref, p * ND * MSG)

        def per_col(qq):
            def tile(base, row0, stride):
                return lambda t: fw_ref[
                    pl.ds((t // THIRD) * ND * MSG + base * MSG + row0 + t % THIRD, 8, stride=stride), :
                ]

            rows = range(12 * p, 12 * p + 12)
            low = split_rows(tile(qq * NR, 0, MSG), rows)
            high = split_rows(tile(qq * NR + 8, 0, MSG), rows)
            for (ii, a), (_, b) in zip(low, high):
                put16(l_ref, ii, q_lanes(qq), a, b)
            for h in range(2):
                for jj, v in split_rows(tile(qq * NR + h, THIRD, 2 * MSG), rows):
                    rf_ref[pl.ds(qq * KP + h * TI + jj, 8, stride=128), :] = v
            if p == 2:
                r_ref[:, q_lanes(qq)] = rf_ref[pl.ds(pl.multiple_of(qq * KP, KP), KP), :].astype(BF)

        chunks(NQ, per_col)

    m_parts = ((0, A_ROWS, 0, 8, s_m0, r_m0), (A_ROWS, TI, 8, NT, s_m1, r_m1))
    for k, (i0, i1, t0, t1, src, dst) in enumerate(m_parts):
        rows = slice(i0 * NR, i1 * NR)
        size = src.shape[1]
        for b in range(0, KP, 256):
            c1_ref[rows, b : b + 256] = mm_nt(l_ref[rows, :], r_ref[b : b + 256, :])

        def pack(qq):
            for h in range(2):
                row = lambda ii: c1_ref[ii * NR + 8 * h : ii * NR + 8 * h + 8, q_lanes(qq)]
                for t, v in join_rows(row, range(t0, t1)):
                    f_ref[pl.ds((qq * NR + 8 * h) * size + t - t0, 8, stride=size), :] = v

        chunks(NQ, pack)
        narrow(f_ref, src)
        exchange_start(src, dst, by_entry, by_channel, sem_m.at[k])

    def middle(t0, nt, base, size, out0, out_size):
        w = nt * 128
        lanes = slice(t0 * 128, t0 * 128 + w)
        mixed = jnp.concatenate(
            [
                jnp.concatenate(
                    [fw_ref[pl.ds(base + tt + 8 * g * size, 8, stride=size), :] for g in range(C // 8)],
                    axis=0,
                )
                for tt in range(nt)
            ],
            axis=1,
        )
        normed_x, r_x = norm(mixed)
        scaled_out = (normed_x * gain_out()).astype(BF)
        output = mm(owt[...], scaled_out)
        gate = gate_ref[:, lanes]
        after = (xt_ref[:, lanes].astype(F32) + gate * output).astype(BF).astype(F32)
        normed_t, r_t = norm(after)
        scaled_t = (normed_t * gain_t()).astype(BF)
        cot_b = cott_ref[:, lanes]
        hid_ref[:, :w] = mm(tit[...], scaled_t)
        gi_ref[:, :w] = mm(to_ref[...], cot_b)
        for i in range(0, H, 16):
            g = hid_ref[i : i + 16, :w]
            u = hid_ref[H + i : H + i + 16, :w]
            gi = gi_ref[i : i + 16, :w]
            sg = sigmoid(g)
            swish = g * sg
            inner_ref[i : i + 16, :w] = (swish * u).astype(BF)
            gh_ref[i : i + 16, :w] = (gi * u * (sg + swish * (1.0 - sg))).astype(BF)
            gh_ref[H + i : H + i + 16, :w] = (gi * swish).astype(BF)
        back_t = mm(ti_ref[...], gh_ref[:, :w])
        tout_acc[...] += mm_nt(inner_ref[:, :w], cot_b)
        tin_acc[...] += mm_nt(gh_ref[:, :w], scaled_t)
        gn_acc[1] += fold(back_t * normed_t)
        grad_after = cot_b.astype(F32) + norm_back(back_t * gain_t(), normed_t, r_t)
        after_ref[:, lanes] = grad_after
        grad_output = (grad_after * gate).astype(BF)
        grad_logit = (grad_after * output * gate * (1.0 - gate)).astype(BF)
        logit_ref[:, lanes] = grad_logit
        gw_acc[...] += mm_nt(scaled_ref[:, lanes], grad_logit)
        ow_acc[...] += mm_nt(scaled_out, grad_output)
        back_x = mm(ow_ref[...], grad_output)
        gn_acc[0] += fold(back_x * normed_x)
        grad_mixed = norm_back(back_x * gain_out(), normed_x, r_x)
        for tt in range(nt):
            for g in range(C // 8):
                f_ref[pl.ds(out0 + tt + 8 * g * out_size, 8, stride=out_size), :] = grad_mixed[
                    8 * g : 8 * g + 8, tt * 128 : (tt + 1) * 128
                ]

    exchange_wait(s_m0, r_m0, sem_m.at[0])
    widen(r_m0, fw_ref)
    middle(0, 8, 0, 8, 0, MSG)
    exchange_wait(s_m1, r_m1, sem_m.at[1])
    widen(r_m1, fw_ref)
    middle(8, 5, 0, MSG, 8, MSG)
    narrow(f_ref, s_g0)
    exchange_start(s_g0, r_g0, by_channel, by_entry, sem_g.at[0])
    middle(G_TILES, 8, G_TILES - 8, MSG, 0, 8)
    narrow(f_ref, s_g1)
    exchange_start(s_g1, r_g1, by_channel, by_entry, sem_g.at[1])

    for p in range(3):
        exchange_wait_send(s_a.at[p], r_a.at[p], sem_a.at[p])
    s_b0, s_b1, r_b0, r_b1 = s_a.at[0], s_a.at[1], r_a.at[0], r_a.at[1]
    second = ND * MSG

    def operand(i0, i1):
        def per_col(qq):
            def tile(h):
                first = qq * NR + 8 * h

                def get(t):
                    if t < G_TILES:
                        return fw_ref[pl.ds(first * MSG + t, 8, stride=MSG), :]
                    return fw_ref[pl.ds(second + first * 8 + t - G_TILES, 8, stride=8), :]

                return get

            low, high = split_rows(tile(0), range(i0, i1)), split_rows(tile(1), range(i0, i1))
            for (ii, a), (_, b) in zip(low, high):
                put16(m_ref, ii, q_lanes(qq), a, b)

        chunks(NQ, per_col)
        rows = slice(i0 * NR, i1 * NR)
        for b in range(0, KP, 256):
            c1_ref[rows, b : b + 256] = mm(m_ref[rows, :], r_ref[:, b : b + 256])

    def pack_left(tiles, row0, size):
        def pack(qq):
            for h in range(2):
                row = lambda ii: c1_ref[ii * NR + 8 * h : ii * NR + 8 * h + 8, q_lanes(qq)]
                for t, v in join_rows(row, tiles):
                    f_ref[pl.ds((qq * NR + 8 * h) * size + row0 + t - tiles[0], 8, stride=size), :] = v

        chunks(NQ, pack)

    def pack_right(tiles, row0, size):
        def pack(qq):
            for h in range(2):
                row = lambda jj: rf_ref[pl.ds(qq * KP + h * TI + jj, 8, stride=128), :]
                for t, v in join_rows(row, tiles):
                    at = pl.ds((qq * NR + h) * size + row0 + t - tiles[0], 8, stride=2 * size)
                    f_ref[at, :] = v

        chunks(NQ, pack)

    exchange_wait(s_g0, r_g0, sem_g.at[0])
    widen(r_g0, fw_ref)
    operand(0, G_ROWS)
    pack_left(range(0, 12), 0, MSG)
    narrow(f_ref, s_b0)
    exchange_start(s_b0, r_b0, by_entry, by_channel, sem_b.at[0])

    def put_terms(dst, first, value):
        n = value.shape[0] // MSG
        dst[first // MSG : first // MSG + n] = value.astype(BF).reshape(n, MSG, 128)

    def gain_rows(values):
        rows = [jnp.sum(v.T, axis=0, keepdims=True) for v in values]
        return jnp.concatenate(rows + [jnp.zeros((MSG - len(rows), 128), F32)], axis=0)

    put_terms(s_mid, 0, tin_acc[...])
    put_terms(s_mid, 2 * H, tout_acc[...])
    put_terms(s_mid, 3 * H, ow_acc[...])
    put_terms(s_mid, 3 * H + C, gw_acc[...])
    rest = 3 * H + 2 * C
    put_terms(s_mid, rest, gain_rows([gn_acc[0], gn_acc[1]]))
    s_mid[rest // MSG + 1 :] = jnp.zeros((ND - rest // MSG - 1, MSG, 128), BF)
    exchange_start(s_mid, r_mid, by_channel, by_channel, sem_mid)

    exchange_wait(s_g1, r_g1, sem_g.at[1])
    widen(r_g1, fw_ref, second)
    operand(G_ROWS, TI)
    for b in range(0, KP, 128):
        mt_ref[b : b + 128, :] = mm_nt(eye(), m_ref[:, b : b + 128]).astype(BF)
    for b in range(0, KP, 256):
        both = mm(mt_ref[...], l_ref[:, b : b + 256])
        rf_ref[b // 128 * KP : (b // 128 + 1) * KP, :] = both[:, :128]
        rf_ref[(b // 128 + 1) * KP : (b // 128 + 2) * KP, :] = both[:, 128:]
    pack_left(range(12, NT), 0, MSG)
    pack_right(range(0, 7), 9, MSG)
    narrow(f_ref, s_b1)
    exchange_start(s_b1, r_b1, by_entry, by_channel, sem_b.at[1])
    pack_right(range(7, 15), 0, 8)
    narrow(f_ref, s_b2)
    exchange_start(s_b2, r_b2, by_entry, by_channel, sem_b.at[2])
    pack_right(range(15, NT), 0, 8)
    narrow(f_ref, s_b3)
    exchange_start(s_b3, r_b3, by_entry, by_channel, sem_b.at[3])

    def spread(own, dst, slot, sems):
        def send(pr, pq):
            pltpu.make_async_remote_copy(
                src_ref=own,
                dst_ref=dst.at[slot],
                send_sem=sems.at[0],
                recv_sem=sems.at[1],
                device_id=(pr, pq),
                device_id_type=MESH,
            ).start()

        each_peer(send)
        pltpu.make_async_copy(own, dst.at[slot], sems.at[2]).start()

    exchange_wait(s_mid, r_mid, sem_mid)
    mid_own[...] = sum_blocks(r_mid).astype(BF)
    spread(mid_own, mid_sum, me, sem_mid2)

    def left_at(t):
        return (t, MSG) if t < 12 else (second + t - 12, MSG)

    def right_at(t):
        if t < 7:
            return (second + 9 + t, MSG)
        return (2 * second + t - 7, 8) if t < 15 else (2 * second + ND * 8 + t - 15, 8)

    def project_back(t0, nt):
        w = nt * 128
        lanes = slice(t0 * 128, t0 * 128 + w)
        live = live_ref[0:1, lanes]
        for i in range(0, C, 16):
            for k, at in ((0, left_at), (2, right_at)):
                grad = []
                for t in range(t0, t0 + nt):
                    base, size = at(t)
                    grad.append(
                        jnp.concatenate(
                            [fw_ref[pl.ds(base + (i + 8 * g) * size, 8, stride=size), :] for g in range(2)],
                            axis=0,
                        )
                    )
                s = sigmoid(proj_ref[k * C + i : k * C + i + 16, lanes])
                gs = live * jnp.concatenate(grad, axis=1) * s
                gp_ref[(k + 1) * C + i : (k + 1) * C + i + 16, :w] = gs.astype(BF)
                gp_ref[k * C + i : k * C + i + 16, :w] = (
                    gs * proj_ref[(k + 1) * C + i : (k + 1) * C + i + 16, lanes] * (1.0 - s)
                ).astype(BF)
        normed, inverse = norm(xt_ref[:, lanes].astype(F32))
        pw_acc[...] += mm_nt(gp_ref[:, :w], scaled_ref[:, lanes])
        back = mm(pw_ref[...], gp_ref[:, :w]) + mm(gw_ref[...], logit_ref[:, lanes])
        gn_acc[2] += fold(back * normed)
        after_ref[:, lanes] += norm_back(back * gain_in(), normed, inverse)

    exchange_wait(s_b0, r_b0, sem_b.at[0])
    widen(r_b0, fw_ref)
    exchange_wait(s_b1, r_b1, sem_b.at[1])
    widen(r_b1, fw_ref, second)
    project_back(0, 7)
    exchange_wait(s_b2, r_b2, sem_b.at[2])
    widen(r_b2, fw_ref, 2 * second)
    project_back(7, 8)
    exchange_wait(s_b3, r_b3, sem_b.at[3])
    widen(r_b3, fw_ref, 2 * second + ND * 8)
    project_back(15, 6)

    put_terms(s_tail, 0, pw_acc[...])
    put_terms(s_tail, 4 * C, gain_rows([gn_acc[2]]))
    even = lax.rem(r, 4) == 0
    odd_one = jnp.logical_and(r == 2, q == 0)
    owner = jnp.logical_or(even, odd_one)
    my_part = jnp.where(even, (r // 4) * NQ + q, OWNERS - 1)

    def tail_send(o, pr, pq):
        remote = jnp.logical_or(pr != r, pq != q)

        @pl.when(remote)
        def _():
            pltpu.make_async_remote_copy(
                src_ref=s_tail.at[o],
                dst_ref=r_tail.at[me],
                send_sem=sem_tail.at[0],
                recv_sem=sem_tail.at[1],
                device_id=(pr, pq),
                device_id_type=MESH,
            ).start()

        @pl.when(jnp.logical_not(remote))
        def _():
            pltpu.make_async_copy(s_tail.at[o], r_tail.at[me], sem_tail.at[2]).start()

    def four(i, carry):
        for k in range(NQ):
            tail_send(i * NQ + k, 4 * i, k)
        return carry

    lax.fori_loop(0, 4, four, 0)
    tail_send(OWNERS - 1, 2, 0)

    for t0 in range(0, NT, 3):
        stop = min((t0 + 3) * 128, E)
        pair_o[t0 * 128 : stop, :] = after_ref[:, t0 * 128 : t0 * 128 + 384].T[: stop - t0 * 128].astype(BF)

    @pl.when(owner)
    def _():
        exchange_wait(r_tail, r_tail, sem_tail)
        tail_own[...] = sum_blocks(r_tail).astype(BF)
        spread(tail_own, tail_sum, my_part, sem_tail2)

    exchange_wait(r_mid, mid_sum, sem_mid2)
    def tail_wait(n):
        pltpu.make_async_copy(r_tail.at[pl.ds(0, n)], r_tail.at[pl.ds(0, n)], sem_tail2.at[1]).wait()

    @pl.when(owner)
    def _():
        tail_wait(OWNERS - 1)
        pltpu.make_async_copy(tail_own, tail_sum.at[0], sem_tail2.at[2]).wait()

    @pl.when(jnp.logical_not(owner))
    def _():
        tail_wait(OWNERS)

    for k, (src, dst) in enumerate(((s_m0, r_m0), (s_m1, r_m1))):
        exchange_wait_send(src, dst, sem_m.at[k])
    for k, (src, dst) in enumerate(((s_g0, r_g0), (s_g1, r_g1))):
        exchange_wait_send(src, dst, sem_g.at[k])
    for k, (src, dst) in enumerate(((s_b0, r_b0), (s_b1, r_b1), (s_b2, r_b2), (s_b3, r_b3))):
        exchange_wait_send(src, dst, sem_b.at[k])
    exchange_wait_send(s_mid, r_mid, sem_mid)
    exchange_wait_send(r_mid, mid_sum, sem_mid2)

    def tail_left(n, sem):
        pltpu.make_async_copy(r_tail.at[pl.ds(0, n)], r_tail.at[pl.ds(0, n)], sem).wait()

    @pl.when(owner)
    def _():
        tail_left(OWNERS - 1, sem_tail.at[0])
        tail_left(ND - 1, sem_tail2.at[0])

    @pl.when(jnp.logical_not(owner))
    def _():
        tail_left(OWNERS, sem_tail.at[0])


def block(x, cot, live, pw, gw, ow, ti, to, gains):
    H = to.shape[0]
    wide = 1024
    msgs = lambda rows, *lead: pltpu.VMEM((*lead, ND, rows, 128), BF)
    dma = lambda *shape: pltpu.SemaphoreType.DMA(shape)
    v = pltpu.VMEM
    return pl.pallas_call(
        block_kernel,
        out_shape=(sds((E, C), BF), sds((ND, *BLK), BF), sds((OWNERS, *BLK), BF)),
        in_specs=vspec(9),
        out_specs=tuple(vspec(3)),
        scratch_shapes=[
            v((4 * C, C), BF), v((C, C), BF), v((C, C), BF), v((2 * H, C), BF), v((C, C), F32),
            v((C, EP), BF), v((C, EP), BF), v((C, EP), BF), v((4 * C, EP), F32), v((C, EP), F32),
            v((C, EP), F32), v((C, EP), BF),
            v((ND * MSG, 128), F32), v((3 * ND * MSG, 128), F32),
            v((MROWS, KP), BF), v((KP, KP), BF), v((NQ * KP, 128), F32), v((MROWS, KP), BF),
            v((KP, MROWS), BF), v((MROWS, KP), F32),
            v((2 * H, wide), F32), v((H, wide), F32), v((H, wide), BF), v((2 * H, wide), BF),
            v((4 * C, wide), BF),
            v((2 * H, C), F32), v((H, C), F32), v((C, C), F32), v((C, C), F32), v((4 * C, C), F32),
            v((3, C, 128), F32),
            msgs(16, 3), msgs(16, 3), msgs(8), msgs(8), msgs(16), msgs(16), msgs(16), msgs(16),
            msgs(8), msgs(8), msgs(8), msgs(8), msgs(8), msgs(8),
            msgs(16), msgs(16), v(BLK, BF),
            v((OWNERS, *BLK), BF), msgs(16), v(BLK, BF),
            dma(3, 3), dma(2, 3), dma(2, 3), dma(4, 3), dma(3), dma(3), dma(3), dma(3),
            pltpu.SemaphoreType.REGULAR,
        ],
        compiler_params=pltpu.CompilerParams(
            collective_id=1, has_side_effects=True, vmem_limit_bytes=VMEM_LIMIT
        ),
        name="block",
    )(x, cot, live, pw, gw, ow, ti, to, gains)


def finish_kernel(pair_ref, mid_ref, tail_ref, pair_o, pw_o, gw_o, ow_o, ti_o, to_o, gn_o):
    H = to_o.shape[0]
    scale = 1.0 / (TI * NR)

    def total(ref, first, rows):
        return ref[first // MSG : (first + rows) // MSG].astype(F32).reshape(rows, 128) * scale

    pair_o[...] = pair_ref[...]
    for b in range(0, 2 * H, C):
        ti_o[:, b : b + C] = total(mid_ref, b, C).T
    to_o[...] = total(mid_ref, 2 * H, H)
    ow_o[...] = total(mid_ref, 3 * H, C)
    gw_o[...] = total(mid_ref, 3 * H + C, C)
    for b in range(0, 4 * C, C):
        pw_o[:, b : b + C] = total(tail_ref, b, C).T
    gn_o[...] = jnp.concatenate(
        [total(tail_ref, 4 * C, MSG)[0:1], total(mid_ref, 3 * H + 2 * C, MSG)[0:2]], axis=0
    )


def finish(pair, mid, tail, pw, gw, ow, ti, to, gains):
    return pl.pallas_call(
        finish_kernel,
        out_shape=(
            sds((E, C), BF), sds(pw.shape, F32), sds(gw.shape, F32), sds(ow.shape, F32),
            sds(ti.shape, F32), sds(to.shape, F32), sds(gains.shape, F32),
        ),
        in_specs=vspec(3),
        out_specs=tuple(vspec(7)),
        name="finish",
    )(pair, mid, tail)


def on_device(
    pair_act, cotangent, residue_mask, pair_mask, proj_weight, gate_weight, out_weight,
    trans_in, trans_out, norm_gains,
):
    live_res = residue_mask.astype(F32)
    row_live = lax.dynamic_slice_in_dim(live_res, lax.axis_index("row") * TI, TI)
    col_live = lax.dynamic_slice_in_dim(live_res, lax.axis_index("col") * TK, TK)
    live = pair_mask.astype(F32) * row_live[:, None] * col_live[None, :]
    live = jnp.pad(live.reshape(1, E), ((0, 7), (0, EP - E)))
    weights = (proj_weight, gate_weight, out_weight, trans_in, trans_out, norm_gains)
    sums = block(pair_act.reshape(E, C), cotangent.reshape(E, C), live, *weights)
    out = finish(*sums, *weights)
    return (out[0].reshape(TI, TK, C), *out[1:])


def solution(mesh):
    split = P("row", "col", None)
    in_specs = (split, split, P(), P("row", "col"), P(), P(), P(), P(), P(), P())
    out_specs = (split, P(), P(), P(), P(), P(), P())
    return jax.shard_map(
        on_device, mesh=mesh, in_specs=in_specs, out_specs=out_specs, check_vma=False
    )
```

time: 126 us -> 117 us (0.929)
  local copies, waits for them, and re-layouts: 8.18 us -> 1.58 us
  Pallas kernels: 117 us -> 115 us
    unnamed x23 -> x4, local copies, waits for them, and re-layouts: 7.29 us -> 0.69 us
    pallas_call x1 -> x2, Pallas kernels: 117 us -> 115 us  [the longest x1 112 us: block(): pl.pallas_call(block_kernel, out_shape=(sds((E, C), BF), sds((ND, *BLK),...]
where the time goes in v3:
time: 117 us
  Pallas kernels  115 us (98%)
  local copies, waits for them, and re-layouts  1.58 us (1%)
    pallas_call x1, Pallas kernels, block(): pl.pallas_call(block_kernel, out_shape=(sds((E, C), BF), sds((ND, *BLK),...  112 us
    pallas_call x1, Pallas kernels, finish(): pl.pallas_call(finish_kernel, out_shape=(sds((E, C), BF), sds(pw.shape, F...  2.69 us

profile of v3, /device:TPU:1, one launch (start us, length us, event | category | flops | bytes accessed | tf_op | source)
XLA Modules:
  0.0 116.9 jit_solution(1061202326975552717)
XLA Ops:
  0.6 0.0 copy-start
  0.6 0.0 copy-start.1
  0.7 0.7 copy-done.1
  1.3 0.1 dynamic_slice.7
  1.4 0.1 dynamic_slice.6
  1.5 0.0 copy-done
  1.5 0.1 multiply_multiply_fusion
  1.6 0.1 reshape.30
  1.7 0.6 pad.4.live_ref
  2.3 111.9 %block.1 = (bf16[2592,128]{1,0:T(8,128)(2,1)}, bf16[128,16,128]{2,1,0:T(8,128)(2,1)}, bf16[33,16,128]{2,1,0:T(8,128)(2,1)}) custom-call(bf16[2592,128]{1,0:T(8,128)(2,1)} %bitcast.3, bf16[2592,128]{1,0:T(8,128)(2,1)} %bitcast.4, f32[8,2688]{1,0:T(8,128)} %pad.4.live_ref, bf16[128,512]{1,0:T(8,128)(2,1)} %pw_ref.1, bf16[128,128]{1,0:T(8,128)(2,1)} %gw_ref.1, ...), custom_call_target="tpu_custom_call" | custom-call | tf_op jit(solution)/shard_map/block/pallas_call | solution.py:655
  114.2 2.7 %finish.1 = (bf16[2592,128]{1,0:T(8,128)(2,1)}, f32[128,512]{1,0:T(8,128)}, f32[128,128]{1,0:T(8,128)}, f32[128,128]{1,0:T(8,128)}, f32[128,1024]{1,0:T(8,128)}, /*index=5*/f32[512,128]{1,0:T(8,128)}, f32[3,128]{1,0:T(4,128)}) custom-call(bf16[2592,128]{1,0:T(8,128)(2,1)} %get-tuple-element.17.pair_ref, bf16[128,16,128]{2,1,0:T(8,128)(2,1)} %get-tuple-element.18.mid_ref, ...), custom_call_target="tpu_custom_call" | custom-call | tf_op jit(solution)/shard_map/finish/pallas_call | solution.py:706
  (1 shorter events, 0.0 us)
Async XLA Ops:
  0.6 0.9 copy-start
  0.6 0.7 copy-start.1

commit v4 on v3

--- a/solution.py
+++ b/solution.py
@@ -21,11 +21,10 @@
 MROWS = TI * NR
 KP = NQ * 128
 MSG = 16
-BLK = (MSG, 128)
+HALF = ND // 2
 G_TILES, G_ROWS = 13, 23
 A_ROWS = 16
 THIRD = 7
-OWNERS = 33
 VMEM_LIMIT = 60 * 2**20
 
 
@@ -70,8 +69,10 @@
 def each_peer(fn):
     r, q = lax.axis_index("row"), lax.axis_index("col")
 
+    cols = [lax.rem(q + dq, NQ) for dq in range(NQ)]
+
     def one(pr, dq):
-        fn(pr, lax.rem(q + dq, NQ))
+        fn(pr, cols[dq])
 
     for dq in range(1, NQ):
         one(r, dq)
@@ -212,13 +213,11 @@
     return sum(v[:, k : k + 128] for k in range(128, v.shape[1], 128)) + v[:, :128]
 
 
-def sum_blocks(ref):
-    def some(i, acc):
-        for k in range(8):
-            acc = acc + ref[i * 8 + k].astype(F32)
-        return acc
-
-    return lax.fori_loop(0, ND // 8, some, jnp.zeros(BLK, F32))
+def add_blocks(ref, dst):
+    total = ref[0].astype(F32)
+    for k in range(1, ref.shape[0]):
+        total = total + ref[k].astype(F32)
+    dst[...] = total.astype(BF)
 
 
 def block_kernel(
@@ -228,9 +227,9 @@
     after_ref, logit_ref, f_ref, fw_ref, l_ref, r_ref, rf_ref, m_ref, mt_ref, c1_ref,
     hid_ref, gi_ref, inner_ref, gh_ref, gp_ref, tin_acc, tout_acc, ow_acc, gw_acc, pw_acc, gn_acc,
     s_a, r_a, s_m0, r_m0, s_m1, r_m1, s_g0, r_g0, s_g1, r_g1, s_b2, r_b2, s_b3, r_b3,
-    s_mid, r_mid, mid_own,
-    s_tail, r_tail, tail_own,
-    sem_a, sem_m, sem_g, sem_b, sem_mid, sem_mid2, sem_tail, sem_tail2, entered,
+    s_mid, h_mid, p_mid, r_mid, own_mid,
+    s_tail, r_tail, row_tail, q_tail, all_tail,
+    sem_a, sem_m, sem_g, sem_b, sem_mid, sem_tail, entered,
 ):
     H = to_ref.shape[0]
     r, q = lax.axis_index("row"), lax.axis_index("col")
@@ -466,9 +465,13 @@
     narrow(f_ref, s_b0)
     exchange_start(s_b0, r_b0, by_entry, by_channel, sem_b.at[0])
 
+    core, chip = lax.rem(r, 2), (r // 2) * NQ + q
+    sibling = r + 1 - 2 * core
+
     def put_terms(dst, first, value):
+        half, at = divmod(first // MSG, HALF)
         n = value.shape[0] // MSG
-        dst[first // MSG : first // MSG + n] = value.astype(BF).reshape(n, MSG, 128)
+        dst[half, at : at + n] = value.astype(BF).reshape(n, MSG, 128)
 
     def gain_rows(values):
         rows = [jnp.sum(v.T, axis=0, keepdims=True) for v in values]
@@ -478,11 +481,76 @@
     put_terms(s_mid, 2 * H, tout_acc[...])
     put_terms(s_mid, 3 * H, ow_acc[...])
     put_terms(s_mid, 3 * H + C, gw_acc[...])
-    rest = 3 * H + 2 * C
-    put_terms(s_mid, rest, gain_rows([gn_acc[0], gn_acc[1]]))
-    s_mid[rest // MSG + 1 :] = jnp.zeros((ND - rest // MSG - 1, MSG, 128), BF)
-    exchange_start(s_mid, r_mid, by_channel, by_channel, sem_mid)
-
+    put_terms(s_mid, 3 * H + 2 * C, gain_rows([gn_acc[0], gn_acc[1]]))
+    rest = (3 * H + 2 * C) // MSG - HALF + 1
+    s_mid[1, rest:] = jnp.zeros((HALF - rest, MSG, 128), BF)
+
+    def to_sibling(src, dst, sems):
+        return pltpu.make_async_remote_copy(
+            src_ref=src,
+            dst_ref=dst,
+            send_sem=sems.at[0],
+            recv_sem=sems.at[1],
+            device_id=(sibling, q),
+            device_id_type=MESH,
+        )
+
+    def same_core(src, dst, sems, pick):
+        cols = [lax.rem(q + d, NQ) for d in range(NQ)]
+
+        def send(pr, pq):
+            pltpu.make_async_remote_copy(
+                src_ref=src.at[(pr // 2) * NQ + pq] if pick else src,
+                dst_ref=dst.at[chip],
+                send_sem=sems.at[0],
+                recv_sem=sems.at[1],
+                device_id=(pr, pq),
+                device_id_type=MESH,
+            ).start()
+
+        for d in range(1, NQ):
+            send(r, cols[d])
+
+        def rows(k):
+            for d in range(NQ):
+                send(lax.rem(r + 2 * (k + 1), NR), cols[d])
+
+        chunks(NR // 2 - 1, rows)
+        pltpu.make_async_copy(src.at[chip] if pick else src, dst.at[chip], sems.at[2]).start()
+
+    def along(axis, src, dst, sems, pick):
+        n, at = (NR, r) if axis == "row" else (NQ, q)
+        for d in range(1, n):
+            peer = lax.rem(at + d, n)
+            pltpu.make_async_remote_copy(
+                src_ref=src.at[peer] if pick else src,
+                dst_ref=dst.at[at],
+                send_sem=sems.at[0],
+                recv_sem=sems.at[1],
+                device_id=(peer, q) if axis == "row" else (r, peer),
+                device_id_type=MESH,
+            ).start()
+        pltpu.make_async_copy(src.at[at] if pick else src, dst.at[at], sems.at[2]).start()
+
+    def along_wait(dst, sems):
+        part = dst.at[pl.ds(0, dst.shape[0] - 1)]
+        pltpu.make_async_copy(part, part, sems.at[1]).wait()
+        pltpu.make_async_copy(dst.at[0], dst.at[0], sems.at[2]).wait()
+
+    def along_wait_send(dst, sems):
+        part = dst.at[pl.ds(0, dst.shape[0] - 1)]
+        pltpu.make_async_copy(part, part, sems.at[0]).wait()
+
+    to_sibling(s_mid.at[1 - core], h_mid, sem_mid.at[0]).start()
+
+    to_sibling(s_mid.at[1 - core], h_mid, sem_mid.at[0]).wait()
+
+    def pair_sum(i):
+        at = pl.ds(i * 16, 16)
+        p_mid[at] = (s_mid[core, at].astype(F32) + h_mid[at].astype(F32)).astype(BF)
+
+    chunks(HALF // 16, pair_sum)
+    same_core(p_mid, r_mid, sem_mid.at[1], True)
     exchange_wait(s_g1, r_g1, sem_g.at[1])
     widen(r_g1, fw_ref, second)
     operand(G_ROWS, TI)
@@ -503,23 +571,9 @@
     narrow(f_ref, s_b3)
     exchange_start(s_b3, r_b3, by_entry, by_channel, sem_b.at[3])
 
-    def spread(own, dst, slot, sems):
-        def send(pr, pq):
-            pltpu.make_async_remote_copy(
-                src_ref=own,
-                dst_ref=dst.at[slot],
-                send_sem=sems.at[0],
-                recv_sem=sems.at[1],
-                device_id=(pr, pq),
-                device_id_type=MESH,
-            ).start()
-
-        each_peer(send)
-        pltpu.make_async_copy(own, dst.at[slot], sems.at[2]).start()
-
-    exchange_wait(s_mid, r_mid, sem_mid)
-    mid_own[...] = sum_blocks(r_mid).astype(BF)
-    spread(mid_own, mid_sum, me, sem_mid2)
+    along_wait(r_mid, sem_mid.at[1])
+    add_blocks(r_mid, own_mid)
+    same_core(own_mid, mid_sum.at[core], sem_mid.at[2], False)
 
     def left_at(t):
         return (t, MSG) if t < 12 else (second + t - 12, MSG)
@@ -568,61 +622,35 @@
     widen(r_b3, fw_ref, 2 * second + ND * 8)
     project_back(15, 6)
 
-    put_terms(s_tail, 0, pw_acc[...])
-    put_terms(s_tail, 4 * C, gain_rows([gn_acc[2]]))
-    even = lax.rem(r, 4) == 0
-    odd_one = jnp.logical_and(r == 2, q == 0)
-    owner = jnp.logical_or(even, odd_one)
-    my_part = jnp.where(even, (r // 4) * NQ + q, OWNERS - 1)
-
-    def tail_send(o, pr, pq):
-        remote = jnp.logical_or(pr != r, pq != q)
-
-        @pl.when(remote)
-        def _():
-            pltpu.make_async_remote_copy(
-                src_ref=s_tail.at[o],
-                dst_ref=r_tail.at[me],
-                send_sem=sem_tail.at[0],
-                recv_sem=sem_tail.at[1],
-                device_id=(pr, pq),
-                device_id_type=MESH,
-            ).start()
-
-        @pl.when(jnp.logical_not(remote))
-        def _():
-            pltpu.make_async_copy(s_tail.at[o], r_tail.at[me], sem_tail.at[2]).start()
-
-    def four(i, carry):
-        for k in range(NQ):
-            tail_send(i * NQ + k, 4 * i, k)
-        return carry
-
-    lax.fori_loop(0, 4, four, 0)
-    tail_send(OWNERS - 1, 2, 0)
-
-    for t0 in range(0, NT, 3):
+    own_rows = 4 * C // NR
+    s_tail[:, 0:own_rows, :] = pw_acc[...].astype(BF).reshape(NR, own_rows, 128)
+    last_gain = gain_rows([gn_acc[2]]).astype(BF)
+    for k in range(NR):
+        s_tail[k, own_rows : own_rows + MSG, :] = last_gain
+    along("row", s_tail, r_tail, sem_tail.at[0], True)
+
+    def pair_rows(t0):
         stop = min((t0 + 3) * 128, E)
         pair_o[t0 * 128 : stop, :] = after_ref[:, t0 * 128 : t0 * 128 + 384].T[: stop - t0 * 128].astype(BF)
 
-    @pl.when(owner)
-    def _():
-        exchange_wait(r_tail, r_tail, sem_tail)
-        tail_own[...] = sum_blocks(r_tail).astype(BF)
-        spread(tail_own, tail_sum, my_part, sem_tail2)
-
-    exchange_wait(r_mid, mid_sum, sem_mid2)
-    def tail_wait(n):
-        pltpu.make_async_copy(r_tail.at[pl.ds(0, n)], r_tail.at[pl.ds(0, n)], sem_tail2.at[1]).wait()
-
-    @pl.when(owner)
-    def _():
-        tail_wait(OWNERS - 1)
-        pltpu.make_async_copy(tail_own, tail_sum.at[0], sem_tail2.at[2]).wait()
-
-    @pl.when(jnp.logical_not(owner))
-    def _():
-        tail_wait(OWNERS)
+    pair_rows(0)
+    pair_rows(3)
+    along_wait(r_tail, sem_tail.at[0])
+    add_blocks(r_tail, row_tail)
+    along("col", row_tail, q_tail, sem_tail.at[1], False)
+    along_wait(mid_sum.at[core], sem_mid.at[2])
+    to_sibling(mid_sum.at[core], mid_sum.at[core], sem_mid.at[3]).start()
+    pair_rows(6)
+    pair_rows(9)
+    pair_rows(12)
+    along_wait(q_tail, sem_tail.at[1])
+    add_blocks(q_tail, all_tail)
+    along("row", all_tail, tail_sum, sem_tail.at[2], False)
+    pair_rows(15)
+    pair_rows(18)
+    to_sibling(mid_sum.at[core], mid_sum.at[core], sem_mid.at[3]).wait()
+    along_wait(tail_sum, sem_tail.at[2])
+
 
     for k, (src, dst) in enumerate(((s_m0, r_m0), (s_m1, r_m1))):
         exchange_wait_send(src, dst, sem_m.at[k])
@@ -630,31 +658,22 @@
         exchange_wait_send(src, dst, sem_g.at[k])
     for k, (src, dst) in enumerate(((s_b0, r_b0), (s_b1, r_b1), (s_b2, r_b2), (s_b3, r_b3))):
         exchange_wait_send(src, dst, sem_b.at[k])
-    exchange_wait_send(s_mid, r_mid, sem_mid)
-    exchange_wait_send(r_mid, mid_sum, sem_mid2)
-
-    def tail_left(n, sem):
-        pltpu.make_async_copy(r_tail.at[pl.ds(0, n)], r_tail.at[pl.ds(0, n)], sem).wait()
-
-    @pl.when(owner)
-    def _():
-        tail_left(OWNERS - 1, sem_tail.at[0])
-        tail_left(ND - 1, sem_tail2.at[0])
-
-    @pl.when(jnp.logical_not(owner))
-    def _():
-        tail_left(OWNERS, sem_tail.at[0])
+    along_wait_send(r_mid, sem_mid.at[1])
+    along_wait_send(mid_sum.at[core], sem_mid.at[2])
+    for k, dst in enumerate((r_tail, q_tail, tail_sum)):
+        along_wait_send(dst, sem_tail.at[k])
 
 
 def block(x, cot, live, pw, gw, ow, ti, to, gains):
     H = to.shape[0]
     wide = 1024
+    tail = pw.shape[1] // NR + MSG
     msgs = lambda rows, *lead: pltpu.VMEM((*lead, ND, rows, 128), BF)
     dma = lambda *shape: pltpu.SemaphoreType.DMA(shape)
     v = pltpu.VMEM
     return pl.pallas_call(
         block_kernel,
-        out_shape=(sds((E, C), BF), sds((ND, *BLK), BF), sds((OWNERS, *BLK), BF)),
+        out_shape=(sds((E, C), BF), sds((2, HALF, MSG, 128), BF), sds((NR, tail, 128), BF)),
         in_specs=vspec(9),
         out_specs=tuple(vspec(3)),
         scratch_shapes=[
@@ -670,9 +689,11 @@
             v((3, C, 128), F32),
             msgs(16, 3), msgs(16, 3), msgs(8), msgs(8), msgs(16), msgs(16), msgs(16), msgs(16),
             msgs(8), msgs(8), msgs(8), msgs(8), msgs(8), msgs(8),
-            msgs(16), msgs(16), v(BLK, BF),
-            v((OWNERS, *BLK), BF), msgs(16), v(BLK, BF),
-            dma(3, 3), dma(2, 3), dma(2, 3), dma(4, 3), dma(3), dma(3), dma(3), dma(3),
+            v((2, HALF, MSG, 128), BF), v((HALF, MSG, 128), BF), v((HALF, MSG, 128), BF),
+            v((HALF, MSG, 128), BF), v((MSG, 128), BF),
+            v((NR, tail, 128), BF), v((NR, tail, 128), BF), v((tail, 128), BF), v((NQ, tail, 128), BF),
+            v((tail, 128), BF),
+            dma(3, 3), dma(2, 3), dma(2, 3), dma(4, 3), dma(4, 3), dma(3, 3),
             pltpu.SemaphoreType.REGULAR,
         ],
         compiler_params=pltpu.CompilerParams(
@@ -686,20 +707,23 @@
     H = to_o.shape[0]
     scale = 1.0 / (TI * NR)
 
-    def total(ref, first, rows):
-        return ref[first // MSG : (first + rows) // MSG].astype(F32).reshape(rows, 128) * scale
+    def mid(first, rows):
+        half, at = divmod(first // MSG, HALF)
+        return mid_ref[half, at : at + rows // MSG].astype(F32).reshape(rows, 128) * scale
 
     pair_o[...] = pair_ref[...]
     for b in range(0, 2 * H, C):
-        ti_o[:, b : b + C] = total(mid_ref, b, C).T
-    to_o[...] = total(mid_ref, 2 * H, H)
-    ow_o[...] = total(mid_ref, 3 * H, C)
-    gw_o[...] = total(mid_ref, 3 * H + C, C)
-    for b in range(0, 4 * C, C):
-        pw_o[:, b : b + C] = total(tail_ref, b, C).T
-    gn_o[...] = jnp.concatenate(
-        [total(tail_ref, 4 * C, MSG)[0:1], total(mid_ref, 3 * H + 2 * C, MSG)[0:2]], axis=0
-    )
+        ti_o[:, b : b + C] = mid(b, C).T
+    to_o[...] = mid(2 * H, H)
+    ow_o[...] = mid(3 * H, C)
+    gw_o[...] = mid(3 * H + C, C)
+    own_rows = 4 * C // NR
+    blocks = C // own_rows
+    for b in range(4):
+        pw = tail_ref[b * blocks : (b + 1) * blocks, 0:own_rows, :].astype(F32).reshape(C, 128)
+        pw_o[:, b * C : (b + 1) * C] = pw.T * scale
+    last_gain = tail_ref[0, own_rows : own_rows + MSG, :].astype(F32)[0:1] * scale
+    gn_o[...] = jnp.concatenate([last_gain, mid(3 * H + 2 * C, MSG)[0:2]], axis=0)
 
 
 def finish(pair, mid, tail, pw, gw, ow, ti, to, gains):

time: 117 us -> 114 us (0.974)
  Pallas kernels: 115 us -> 111 us
    pallas_call x1, Pallas kernels: 112 us -> 109 us  [block(): pl.pallas_call(block_kernel, out_shape=(sds((E, C), BF), sds((2, HALF, MS...]
where the time goes in v4:
time: 114 us
  Pallas kernels  111 us (97%)
  local copies, waits for them, and re-layouts  1.58 us (1%)
    pallas_call x1, Pallas kernels, block(): pl.pallas_call(block_kernel, out_shape=(sds((E, C), BF), sds((2, HALF, MS...  109 us
    pallas_call x1, Pallas kernels, finish(): pl.pallas_call(finish_kernel, out_shape=(sds((E, C), BF), sds(pw.shape, F...  2.68 us

profile of v4, /device:TPU:1, one launch (start us, length us, event | category | flops | bytes accessed | tf_op | source)
XLA Modules:
  0.0 113.6 jit_solution(5848180417629055490)
XLA Ops:
  0.6 0.0 copy-start
  0.6 0.0 copy-start.1
  0.7 0.7 copy-done.1
  1.3 0.1 dynamic_slice.7
  1.4 0.1 dynamic_slice.6
  1.5 0.0 copy-done
  1.5 0.1 multiply_multiply_fusion
  1.6 0.1 reshape.30
  1.7 0.6 pad.4.live_ref
  2.3 108.6 %block.1 = (bf16[2592,128]{1,0:T(8,128)(2,1)}, bf16[2,64,16,128]{3,2,1,0:T(8,128)(2,1)}, bf16[16,48,128]{2,1,0:T(8,128)(2,1)}) custom-call(bf16[2592,128]{1,0:T(8,128)(2,1)} %bitcast.3, bf16[2592,128]{1,0:T(8,128)(2,1)} %bitcast.4, f32[8,2688]{1,0:T(8,128)} %pad.4.live_ref, bf16[128,512]{1,0:T(8,128)(2,1)} %pw_ref.1, bf16[128,128]{1,0:T(8,128)(2,1)} %gw_ref.1, ...), custom_call_target="tpu_custom_call" | custom-call | tf_op jit(solution)/shard_map/block/pallas_call | solution.py:674
  110.9 2.7 %finish.1 = (bf16[2592,128]{1,0:T(8,128)(2,1)}, f32[128,512]{1,0:T(8,128)}, f32[128,128]{1,0:T(8,128)}, f32[128,128]{1,0:T(8,128)}, f32[128,1024]{1,0:T(8,128)}, /*index=5*/f32[512,128]{1,0:T(8,128)}, f32[3,128]{1,0:T(4,128)}) custom-call(bf16[2592,128]{1,0:T(8,128)(2,1)} %get-tuple-element.17.pair_ref, bf16[2,64,16,128]{3,2,1,0:T(8,128)(2,1)} %get-tuple-element.18.mid_ref, ...), custom_call_target="tpu_custom_call" | custom-call | tf_op jit(solution)/shard_map/finish/pallas_call | solution.py:730
  (1 shorter events, 0.0 us)
Async XLA Ops:
  0.6 0.9 copy-start
  0.6 0.7 copy-start.1

commit v5 on v4

--- a/solution.py
+++ b/solution.py
@@ -22,8 +22,9 @@
 KP = NQ * 128
 MSG = 16
 HALF = ND // 2
-G_TILES, G_ROWS = 13, 23
-A_ROWS = 16
+M_ROWS = 16, 29
+G_ROWS = 14, 28
+AHEAD = 15
 THIRD = 7
 VMEM_LIMIT = 60 * 2**20
 
@@ -226,7 +227,8 @@
     pwt, gwt, owt, tit, gcol, xt_ref, cott_ref, scaled_ref, proj_ref, gate_ref,
     after_ref, logit_ref, f_ref, fw_ref, l_ref, r_ref, rf_ref, m_ref, mt_ref, c1_ref,
     hid_ref, gi_ref, inner_ref, gh_ref, gp_ref, tin_acc, tout_acc, ow_acc, gw_acc, pw_acc, gn_acc,
-    s_a, r_a, s_m0, r_m0, s_m1, r_m1, s_g0, r_g0, s_g1, r_g1, s_b2, r_b2, s_b3, r_b3,
+    s_a, r_a, s_m0, r_m0, s_m1, r_m1, s_m2, r_m2, s_g0, r_g0, s_g1, r_g1, s_g2, r_g2,
+    s_b2, r_b2, s_b3, r_b3,
     s_mid, h_mid, p_mid, r_mid, own_mid,
     s_tail, r_tail, row_tail, q_tail, all_tail,
     sem_a, sem_m, sem_g, sem_b, sem_mid, sem_tail, entered,
@@ -332,7 +334,11 @@
 
         chunks(NQ, per_col)
 
-    m_parts = ((0, A_ROWS, 0, 8, s_m0, r_m0), (A_ROWS, TI, 8, NT, s_m1, r_m1))
+    m_parts = (
+        (0, M_ROWS[0], 0, 8, s_m0, r_m0),
+        (M_ROWS[0], M_ROWS[1], 8, 16, s_m1, r_m1),
+        (M_ROWS[1], TI, 16, NT, s_m2, r_m2),
+    )
     for k, (i0, i1, t0, t1, src, dst) in enumerate(m_parts):
         rows = slice(i0 * NR, i1 * NR)
         size = src.shape[1]
@@ -401,17 +407,14 @@
                     8 * g : 8 * g + 8, tt * 128 : (tt + 1) * 128
                 ]
 
-    exchange_wait(s_m0, r_m0, sem_m.at[0])
-    widen(r_m0, fw_ref)
-    middle(0, 8, 0, 8, 0, MSG)
-    exchange_wait(s_m1, r_m1, sem_m.at[1])
-    widen(r_m1, fw_ref)
-    middle(8, 5, 0, MSG, 8, MSG)
-    narrow(f_ref, s_g0)
-    exchange_start(s_g0, r_g0, by_channel, by_entry, sem_g.at[0])
-    middle(G_TILES, 8, G_TILES - 8, MSG, 0, 8)
-    narrow(f_ref, s_g1)
-    exchange_start(s_g1, r_g1, by_channel, by_entry, sem_g.at[1])
+    third = ND * 8
+    g_parts = ((s_g0, r_g0), (s_g1, r_g1), (s_g2, r_g2))
+    for k, (_, _, t0, t1, src, dst) in enumerate(m_parts):
+        exchange_wait(src, dst, sem_m.at[k])
+        widen(dst, fw_ref, k * third)
+        middle(t0, t1 - t0, k * third, 8, 0, 8)
+        narrow(f_ref, g_parts[k][0])
+        exchange_start(*g_parts[k], by_channel, by_entry, sem_g.at[k])
 
     for p in range(3):
         exchange_wait_send(s_a.at[p], r_a.at[p], sem_a.at[p])
@@ -424,9 +427,7 @@
                 first = qq * NR + 8 * h
 
                 def get(t):
-                    if t < G_TILES:
-                        return fw_ref[pl.ds(first * MSG + t, 8, stride=MSG), :]
-                    return fw_ref[pl.ds(second + first * 8 + t - G_TILES, 8, stride=8), :]
+                    return fw_ref[pl.ds((t // 8) * third + first * 8 + t % 8, 8, stride=8), :]
 
                 return get
 
@@ -460,8 +461,11 @@
 
     exchange_wait(s_g0, r_g0, sem_g.at[0])
     widen(r_g0, fw_ref)
-    operand(0, G_ROWS)
-    pack_left(range(0, 12), 0, MSG)
+    operand(0, G_ROWS[0])
+    exchange_wait(s_g1, r_g1, sem_g.at[1])
+    widen(r_g1, fw_ref, third)
+    operand(G_ROWS[0], G_ROWS[1])
+    pack_left(range(0, AHEAD), 0, MSG)
     narrow(f_ref, s_b0)
     exchange_start(s_b0, r_b0, by_entry, by_channel, sem_b.at[0])
 
@@ -551,23 +555,23 @@
 
     chunks(HALF // 16, pair_sum)
     same_core(p_mid, r_mid, sem_mid.at[1], True)
-    exchange_wait(s_g1, r_g1, sem_g.at[1])
-    widen(r_g1, fw_ref, second)
-    operand(G_ROWS, TI)
+    exchange_wait(s_g2, r_g2, sem_g.at[2])
+    widen(r_g2, fw_ref, 2 * third)
+    operand(G_ROWS[1], TI)
     for b in range(0, KP, 128):
         mt_ref[b : b + 128, :] = mm_nt(eye(), m_ref[:, b : b + 128]).astype(BF)
     for b in range(0, KP, 256):
         both = mm(mt_ref[...], l_ref[:, b : b + 256])
         rf_ref[b // 128 * KP : (b // 128 + 1) * KP, :] = both[:, :128]
         rf_ref[(b // 128 + 1) * KP : (b // 128 + 2) * KP, :] = both[:, 128:]
-    pack_left(range(12, NT), 0, MSG)
-    pack_right(range(0, 7), 9, MSG)
+    pack_left(range(AHEAD, NT), 0, MSG)
+    pack_right(range(0, 10), NT - AHEAD, MSG)
     narrow(f_ref, s_b1)
     exchange_start(s_b1, r_b1, by_entry, by_channel, sem_b.at[1])
-    pack_right(range(7, 15), 0, 8)
+    pack_right(range(10, 18), 0, 8)
     narrow(f_ref, s_b2)
     exchange_start(s_b2, r_b2, by_entry, by_channel, sem_b.at[2])
-    pack_right(range(15, NT), 0, 8)
+    pack_right(range(18, NT), 0, 8)
     narrow(f_ref, s_b3)
     exchange_start(s_b3, r_b3, by_entry, by_channel, sem_b.at[3])
 
@@ -576,12 +580,12 @@
     same_core(own_mid, mid_sum.at[core], sem_mid.at[2], False)
 
     def left_at(t):
-        return (t, MSG) if t < 12 else (second + t - 12, MSG)
+        return (t, MSG) if t < AHEAD else (second + t - AHEAD, MSG)
 
     def right_at(t):
-        if t < 7:
-            return (second + 9 + t, MSG)
-        return (2 * second + t - 7, 8) if t < 15 else (2 * second + ND * 8 + t - 15, 8)
+        if t < 10:
+            return (second + NT - AHEAD + t, MSG)
+        return (2 * second + t - 10, 8) if t < 18 else (2 * second + third + t - 18, 8)
 
     def project_back(t0, nt):
         w = nt * 128
@@ -614,13 +618,13 @@
     widen(r_b0, fw_ref)
     exchange_wait(s_b1, r_b1, sem_b.at[1])
     widen(r_b1, fw_ref, second)
-    project_back(0, 7)
+    project_back(0, 8)
     exchange_wait(s_b2, r_b2, sem_b.at[2])
     widen(r_b2, fw_ref, 2 * second)
-    project_back(7, 8)
+    project_back(8, 8)
     exchange_wait(s_b3, r_b3, sem_b.at[3])
     widen(r_b3, fw_ref, 2 * second + ND * 8)
-    project_back(15, 6)
+    project_back(16, 5)
 
     own_rows = 4 * C // NR
     s_tail[:, 0:own_rows, :] = pw_acc[...].astype(BF).reshape(NR, own_rows, 128)
@@ -652,9 +656,9 @@
     along_wait(tail_sum, sem_tail.at[2])
 
 
-    for k, (src, dst) in enumerate(((s_m0, r_m0), (s_m1, r_m1))):
+    for k, (_, _, _, _, src, dst) in enumerate(m_parts):
         exchange_wait_send(src, dst, sem_m.at[k])
-    for k, (src, dst) in enumerate(((s_g0, r_g0), (s_g1, r_g1))):
+    for k, (src, dst) in enumerate(g_parts):
         exchange_wait_send(src, dst, sem_g.at[k])
     for k, (src, dst) in enumerate(((s_b0, r_b0), (s_b1, r_b1), (s_b2, r_b2), (s_b3, r_b3))):
         exchange_wait_send(src, dst, sem_b.at[k])
@@ -687,13 +691,12 @@
             v((4 * C, wide), BF),
             v((2 * H, C), F32), v((H, C), F32), v((C, C), F32), v((C, C), F32), v((4 * C, C), F32),
             v((3, C, 128), F32),
-            msgs(16, 3), msgs(16, 3), msgs(8), msgs(8), msgs(16), msgs(16), msgs(16), msgs(16),
-            msgs(8), msgs(8), msgs(8), msgs(8), msgs(8), msgs(8),
+            msgs(16, 3), msgs(16, 3), *[msgs(8)] * 16,
             v((2, HALF, MSG, 128), BF), v((HALF, MSG, 128), BF), v((HALF, MSG, 128), BF),
             v((HALF, MSG, 128), BF), v((MSG, 128), BF),
             v((NR, tail, 128), BF), v((NR, tail, 128), BF), v((tail, 128), BF), v((NQ, tail, 128), BF),
             v((tail, 128), BF),
-            dma(3, 3), dma(2, 3), dma(2, 3), dma(4, 3), dma(4, 3), dma(3, 3),
+            dma(3, 3), dma(3, 3), dma(3, 3), dma(4, 3), dma(4, 3), dma(3, 3),
             pltpu.SemaphoreType.REGULAR,
         ],
         compiler_params=pltpu.CompilerParams(

time: 114 us -> 111 us (0.974)
  Pallas kernels: 111 us -> 108 us
    pallas_call x1, Pallas kernels: 109 us -> 105 us  [block(): pl.pallas_call(block_kernel, out_shape=(sds((E, C), BF), sds((2, HALF, MS...]
where the time goes in v5:
time: 111 us; the launch traced here: 110 us
  Pallas kernels  108 us (97%)
  local copies, waits for them, and re-layouts  1.58 us (1%)
    pallas_call x1, Pallas kernels, block(): pl.pallas_call(block_kernel, out_shape=(sds((E, C), BF), sds((2, HALF, MS...  105 us
    pallas_call x1, Pallas kernels, finish(): pl.pallas_call(finish_kernel, out_shape=(sds((E, C), BF), sds(pw.shape, F...  2.68 us

profile of v5, /device:TPU:1, one launch (start us, length us, event | category | flops | bytes accessed | tf_op | source)
XLA Modules:
  0.0 110.4 jit_solution(13421272391487270974)
XLA Ops:
  0.6 0.0 copy-start
  0.6 0.0 copy-start.1
  0.7 0.7 copy-done.1
  1.3 0.1 dynamic_slice.7
  1.4 0.1 dynamic_slice.6
  1.5 0.0 copy-done
  1.5 0.1 multiply_multiply_fusion
  1.6 0.1 reshape.30
  1.7 0.6 pad.4.live_ref
  2.3 105.4 %block.1 = (bf16[2592,128]{1,0:T(8,128)(2,1)}, bf16[2,64,16,128]{3,2,1,0:T(8,128)(2,1)}, bf16[16,48,128]{2,1,0:T(8,128)(2,1)}) custom-call(bf16[2592,128]{1,0:T(8,128)(2,1)} %bitcast.3, bf16[2592,128]{1,0:T(8,128)(2,1)} %bitcast.4, f32[8,2688]{1,0:T(8,128)} %pad.4.live_ref, bf16[128,512]{1,0:T(8,128)(2,1)} %pw_ref.1, bf16[128,128]{1,0:T(8,128)(2,1)} %gw_ref.1, ...), custom_call_target="tpu_custom_call" | custom-call | tf_op jit(solution)/shard_map/block/pallas_call | solution.py:678
  107.7 2.7 %finish.1 = (bf16[2592,128]{1,0:T(8,128)(2,1)}, f32[128,512]{1,0:T(8,128)}, f32[128,128]{1,0:T(8,128)}, f32[128,128]{1,0:T(8,128)}, f32[128,1024]{1,0:T(8,128)}, /*index=5*/f32[512,128]{1,0:T(8,128)}, f32[3,128]{1,0:T(4,128)}) custom-call(bf16[2592,128]{1,0:T(8,128)(2,1)} %get-tuple-element.17.pair_ref, bf16[2,64,16,128]{3,2,1,0:T(8,128)(2,1)} %get-tuple-element.18.mid_ref, ...), custom_call_target="tpu_custom_call" | custom-call | tf_op jit(solution)/shard_map/finish/pallas_call | solution.py:733
  (1 shorter events, 0.0 us)
Async XLA Ops:
  0.6 0.9 copy-start
  0.6 0.7 copy-start.1

commit v6 on v5

--- a/solution.py
+++ b/solution.py
@@ -547,14 +547,6 @@
 
     to_sibling(s_mid.at[1 - core], h_mid, sem_mid.at[0]).start()
 
-    to_sibling(s_mid.at[1 - core], h_mid, sem_mid.at[0]).wait()
-
-    def pair_sum(i):
-        at = pl.ds(i * 16, 16)
-        p_mid[at] = (s_mid[core, at].astype(F32) + h_mid[at].astype(F32)).astype(BF)
-
-    chunks(HALF // 16, pair_sum)
-    same_core(p_mid, r_mid, sem_mid.at[1], True)
     exchange_wait(s_g2, r_g2, sem_g.at[2])
     widen(r_g2, fw_ref, 2 * third)
     operand(G_ROWS[1], TI)
@@ -575,9 +567,14 @@
     narrow(f_ref, s_b3)
     exchange_start(s_b3, r_b3, by_entry, by_channel, sem_b.at[3])
 
-    along_wait(r_mid, sem_mid.at[1])
-    add_blocks(r_mid, own_mid)
-    same_core(own_mid, mid_sum.at[core], sem_mid.at[2], False)
+    to_sibling(s_mid.at[1 - core], h_mid, sem_mid.at[0]).wait()
+
+    def pair_sum(i):
+        at = pl.ds(i * 16, 16)
+        p_mid[at] = (s_mid[core, at].astype(F32) + h_mid[at].astype(F32)).astype(BF)
+
+    chunks(HALF // 16, pair_sum)
+    same_core(p_mid, r_mid, sem_mid.at[1], True)
 
     def left_at(t):
         return (t, MSG) if t < AHEAD else (second + t - AHEAD, MSG)
@@ -622,6 +619,9 @@
     exchange_wait(s_b2, r_b2, sem_b.at[2])
     widen(r_b2, fw_ref, 2 * second)
     project_back(8, 8)
+    along_wait(r_mid, sem_mid.at[1])
+    add_blocks(r_mid, own_mid)
+    same_core(own_mid, mid_sum.at[core], sem_mid.at[2], False)
     exchange_wait(s_b3, r_b3, sem_b.at[3])
     widen(r_b3, fw_ref, 2 * second + ND * 8)
     project_back(16, 5)

time: 111 us -> 113 us (1.018)
  Pallas kernels: 108 us -> 110 us
    pallas_call x1, Pallas kernels: 105 us -> 107 us  [block(): pl.pallas_call(block_kernel, out_shape=(sds((E, C), BF), sds((2, HALF, MS...]
where the time goes in v6:
time: 113 us; the launch traced here: 112 us
  Pallas kernels  110 us (97%)
  local copies, waits for them, and re-layouts  1.58 us (1%)
    pallas_call x1, Pallas kernels, block(): pl.pallas_call(block_kernel, out_shape=(sds((E, C), BF), sds((2, HALF, MS...  107 us
    pallas_call x1, Pallas kernels, finish(): pl.pallas_call(finish_kernel, out_shape=(sds((E, C), BF), sds(pw.shape, F...  2.68 us

profile of v6, /device:TPU:1, one launch (start us, length us, event | category | flops | bytes accessed | tf_op | source)
XLA Modules:
  0.0 112.5 jit_solution(17349339994537937413)
XLA Ops:
  0.6 0.0 copy-start
  0.6 0.0 copy-start.1
  0.7 0.7 copy-done.1
  1.3 0.1 dynamic_slice.7
  1.4 0.1 dynamic_slice.6
  1.5 0.0 copy-done
  1.5 0.1 multiply_multiply_fusion
  1.6 0.1 reshape.30
  1.7 0.6 pad.4.live_ref
  2.3 107.5 %block.1 = (bf16[2592,128]{1,0:T(8,128)(2,1)}, bf16[2,64,16,128]{3,2,1,0:T(8,128)(2,1)}, bf16[16,48,128]{2,1,0:T(8,128)(2,1)}) custom-call(bf16[2592,128]{1,0:T(8,128)(2,1)} %bitcast.3, bf16[2592,128]{1,0:T(8,128)(2,1)} %bitcast.4, f32[8,2688]{1,0:T(8,128)} %pad.4.live_ref, bf16[128,512]{1,0:T(8,128)(2,1)} %pw_ref.1, bf16[128,128]{1,0:T(8,128)(2,1)} %gw_ref.1, ...), custom_call_target="tpu_custom_call" | custom-call | tf_op jit(solution)/shard_map/block/pallas_call | solution.py:678
  109.8 2.7 %finish.1 = (bf16[2592,128]{1,0:T(8,128)(2,1)}, f32[128,512]{1,0:T(8,128)}, f32[128,128]{1,0:T(8,128)}, f32[128,128]{1,0:T(8,128)}, f32[128,1024]{1,0:T(8,128)}, /*index=5*/f32[512,128]{1,0:T(8,128)}, f32[3,128]{1,0:T(4,128)}) custom-call(bf16[2592,128]{1,0:T(8,128)(2,1)} %get-tuple-element.17.pair_ref, bf16[2,64,16,128]{3,2,1,0:T(8,128)(2,1)} %get-tuple-element.18.mid_ref, ...), custom_call_target="tpu_custom_call" | custom-call | tf_op jit(solution)/shard_map/finish/pallas_call | solution.py:733
  (1 shorter events, 0.0 us)
Async XLA Ops:
  0.6 0.9 copy-start
  0.6 0.7 copy-start.1
